TPU v7x, 32 devices: a whole 2x2x4 slice. The times are simulated.
32 devices in a mesh: fsdp: 16 (over z, x, core), seq: 2 (over y).
Axes of the slice: x: 2, y: 2, z: 4, core: 2. Of those that a mesh axis runs over, the one named last changes fastest.
Arguments:
- latents: bfloat16 [16, 1024, 1024], P('fsdp', 'seq'), may hold values from -6 to 6
- cond: bfloat16 [16, 1024], P('fsdp'), may hold values from -6 to 6
- cotangent: bfloat16 [16, 1024, 1024], P('fsdp', 'seq'), may hold values from -6 to 6
- w_qkv: bfloat16 [1024, 3072], P('fsdp'), may hold values from -0.1875 to 0.1875
- w_out: bfloat16 [1024, 1024], P('fsdp'), may hold values from -4 to 4
- w_up: bfloat16 [1024, 4096], P('fsdp', 'seq'), may hold values from -0.1875 to 0.1875
- w_down: bfloat16 [4096, 1024], P('seq', 'fsdp'), may hold values from -0.09375 to 0.09375
- w_ada: bfloat16 [1024, 6144], P(None, 'fsdp'), may hold values from -0.1875 to 0.1875
- b_ada: bfloat16 [6144], P('fsdp'), may hold values from -3 to 3
Outputs:
- mixed: bfloat16 [16, 1024, 1024], P('fsdp', 'seq')
- grad_latents: float32 [16, 1024, 1024], P('fsdp', 'seq')
- grad_cond: float32 [16, 1024], P('fsdp')
- grad_w_qkv: float32 [1024, 3072], P('fsdp')
- grad_w_out: float32 [1024, 1024], P('fsdp')
- grad_w_up: float32 [1024, 4096], P('fsdp', 'seq')
- grad_w_down: float32 [4096, 1024], P('seq', 'fsdp')
- grad_w_ada: float32 [1024, 6144], P(None, 'fsdp')
- grad_b_ada: float32 [6144], P('fsdp')
All inputs are finite; a program needn't handle non-finite values.
Results may differ from a plain program's by a relative error of at most 0.015.
The roundings to bfloat16 on the way count: a program that leaves them out, or rounds other values in their place, can miss the bound.
Values may be sent and summed in bfloat16 or wider, within the bound.
No kernel may reach another device: no remote copies, remote signals or barrier semaphores. Data moves between devices by JAX's collectives and lax.ppermute only.
A program may use at most 128 MiB of HBM per device.

v0:
```python
from functools import partial

import jax
import jax.numpy as jnp
from jax import lax
from jax.experimental import pallas as pl
from jax.experimental.pallas import tpu as pltpu
from jax.sharding import PartitionSpec as P

H = 16
HD = 64
EPSILON = 1e-06
LOG2E = 1.4426950408889634
SCALE2 = HD**-0.5 * LOG2E
MIB = 1024 * 1024
CHUNK = 512
ROOT = 0.7978845608028654
CUBE = 0.044715

NT = (((1,), (1,)), ((), ()))
TN = (((0,), (0,)), ((), ()))
NN = (((1,), (0,)), ((), ()))


def mm(a, b, dims=NN):
    return lax.dot_general(a, b, dims, preferred_element_type=jnp.float32)


def normalize(value_rows):
    center = value_rows - jnp.mean(value_rows, -1, keepdims=True)
    inverse = lax.rsqrt(jnp.mean(center * center, -1, keepdims=True) + EPSILON)
    return (center * inverse, inverse)


def norm_grad(normed, inverse, grad_normed):
    return inverse * (
        grad_normed
        - jnp.mean(grad_normed, -1, keepdims=True)
        - normed * jnp.mean(grad_normed * normed, -1, keepdims=True)
    )


def head_parts(ref, head, rows=slice(None)):
    base = head * 3 * HD
    return [ref[rows, base + j * HD : base + (j + 1) * HD] for j in range(3)]


def attend_kernel(query_ref, all_ref, out_ref, lse_ref):
    rows = query_ref.shape[0]
    for head in range(2):
        _, keys, values = head_parts(all_ref, head)
        chunk = min(CHUNK, rows)
        for at in range(0, rows, chunk):
            span = slice(at, at + chunk)
            queries = head_parts(query_ref, head, span)[0]
            scores = mm(keys, queries, NT)
            highest = jnp.max(scores, 0, keepdims=True)
            raised = jnp.exp2(scores * SCALE2 - highest * SCALE2)
            totals = jnp.sum(raised, 0, keepdims=True)
            result = mm(values, raised.astype(jnp.bfloat16), TN) / totals
            out_ref[span, head * HD : (head + 1) * HD] = result.T.astype(jnp.bfloat16)
            lse_ref[0, head : head + 1, span] = highest * SCALE2 + jnp.log2(totals)


def attend(qkv, tokens, first, count):
    length, columns = qkv.shape
    pairs = columns // (6 * HD)
    return pl.pallas_call(
        attend_kernel,
        grid=(pairs, count),
        in_specs=[
            pl.BlockSpec((tokens, 6 * HD), lambda p, b: (first + b, p)),
            pl.BlockSpec((length, 6 * HD), lambda p, b: (0, p)),
        ],
        out_specs=[
            pl.BlockSpec((tokens, 2 * HD), lambda p, b: (b, p)),
            pl.BlockSpec((1, 2, tokens), lambda p, b: (p, 0, b)),
        ],
        out_shape=[
            jax.ShapeDtypeStruct((count * tokens, pairs * 2 * HD), jnp.bfloat16),
            jax.ShapeDtypeStruct((pairs, 2, count * tokens), jnp.float32),
        ],
        compiler_params=pltpu.CompilerParams(vmem_limit_bytes=24 * MIB),
        cost_estimate=pl.CostEstimate(
            flops=4 * pairs * 2 * HD * length * count * tokens,
            bytes_accessed=0,
            transcendentals=0,
        ),
        name="attend",
    )(qkv, qkv)


def feed_kernel(aliased, hidden_ref, grad_ref, up_ref, down_ref, *rest):
    act_ref, grad_up_ref, branch_ref, part_ref, branch_acc, part_acc = rest[2 * aliased :]
    step = pl.program_id(0)
    up_weights, down_weights = up_ref[...], down_ref[...]
    value = mm(hidden_ref[...], up_weights)
    grad_act = mm(grad_ref[...], down_weights)
    square = value * value
    tanh = jnp.tanh(ROOT * value * (1.0 + CUBE * square))
    half = 0.5 * (1.0 + tanh)
    act = (value * half).astype(jnp.bfloat16)
    slope = half + (0.5 * ROOT) * value * (1.0 - tanh * tanh) * (1.0 + 3.0 * CUBE * square)
    grad_up = (grad_act * slope).astype(jnp.bfloat16)
    act_ref[...] = act
    grad_up_ref[...] = grad_up
    part = mm(grad_up, up_weights, NT)
    branch = mm(act, down_weights, NT)

    @pl.when(step == 0)
    def _():
        part_acc[...] = part
        branch_acc[...] = branch

    @pl.when(step > 0)
    def _():
        part_acc[...] += part
        branch_acc[...] += branch

    @pl.when(step == pl.num_programs(0) - 1)
    def _():
        part_ref[...] = part_acc[...].astype(part_ref.dtype)
        branch_ref[...] = branch_acc[...].astype(branch_ref.dtype)


def feed(hidden, grads_all, up_down, piece, buffers, out_type):
    tokens, width = hidden.shape
    units = up_down.shape[1] // 2
    block = min(512, units)
    count = units // block
    length = grads_all.shape[0]
    rows = pl.BlockSpec((tokens, block), lambda j: (piece, j))
    whole = pl.BlockSpec((tokens, width), lambda j: (0, 0))
    aliased = buffers is not None
    return pl.pallas_call(
        partial(feed_kernel, int(aliased)),
        grid=(count,),
        in_specs=[
            whole,
            pl.BlockSpec((tokens, width), lambda j: (piece, 0)),
            pl.BlockSpec((width, block), lambda j: (0, j)),
            pl.BlockSpec((width, block), lambda j: (0, count + j)),
        ]
        + [pl.BlockSpec(memory_space=pl.ANY)] * (2 * aliased),
        out_specs=[rows, rows, whole, whole],
        out_shape=[jax.ShapeDtypeStruct((length, units), jnp.bfloat16)] * 2
        + [jax.ShapeDtypeStruct((tokens, width), out_type)] * 2,
        scratch_shapes=[pltpu.VMEM((tokens, width), jnp.float32)] * 2,
        input_output_aliases={4: 0, 5: 1} if aliased else {},
        compiler_params=pltpu.CompilerParams(vmem_limit_bytes=40 * MIB),
        cost_estimate=pl.CostEstimate(
            flops=tokens * width * units, bytes_accessed=0, transcendentals=0
        ),
        name="feed",
    )(hidden, grads_all, up_down, up_down, *(buffers or ()))


def turn_kernel(rows, place_ref, value_ref, out_ref):
    at = pl.program_id(0)
    turned = value_ref[...].T
    each = 128 // rows
    for part in range(each):
        start = pl.multiple_of(place_ref[at * each + part] * rows, rows)
        out_ref[pl.ds(start, rows), :] = turned[part * rows : (part + 1) * rows, :]


def turn(value, place):
    length, width = value.shape
    rows = width // place.shape[0]
    return pl.pallas_call(
        partial(turn_kernel, rows),
        grid_spec=pltpu.PrefetchScalarGridSpec(
            num_scalar_prefetch=1,
            grid=(width // 128,),
            in_specs=[pl.BlockSpec((length, 128), lambda b, p: (0, b))],
            out_specs=pl.BlockSpec((width, length), lambda b, p: (0, 0)),
        ),
        out_shape=jax.ShapeDtypeStruct((width, length), value.dtype),
        compiler_params=pltpu.CompilerParams(vmem_limit_bytes=16 * MIB),
        cost_estimate=pl.CostEstimate(flops=0, bytes_accessed=4 * length * width, transcendentals=0),
        name="turn",
    )(place, value)


def hidden_back_kernel(groups, *refs):
    values, (weight_ref, normed_ref, own_ref, peers_ref, sums_ref) = refs[:groups], refs[groups:]
    size = values[0].shape[1]
    tokens = own_ref.shape[0]
    total = mm(values[0][...], weight_ref[:, :size], NT)
    for group in range(1, groups):
        total += mm(values[group][...], weight_ref[:, group * size : (group + 1) * size], NT)
    own_ref[...] = total[:tokens]
    peers_ref[...] = total[tokens:].astype(peers_ref.dtype)
    sums_ref[0:1, :] = jnp.sum(total, 0, keepdims=True)
    sums_ref[1:2, :] = jnp.sum(total * normed_ref[...], 0, keepdims=True)


def hidden_back(values, weights, normed, tokens):
    length, width = normed.shape
    block = min(256, width)
    columns = lambda rows: pl.BlockSpec((rows, block), lambda j: (0, j))
    return pl.pallas_call(
        partial(hidden_back_kernel, len(values)),
        grid=(width // block,),
        in_specs=[pl.BlockSpec(value.shape, lambda j: (0, 0)) for value in values]
        + [pl.BlockSpec((block, weights.shape[1]), lambda j: (j, 0)), columns(length)],
        out_specs=[columns(tokens), columns(length - tokens), columns(2)],
        out_shape=[
            jax.ShapeDtypeStruct((tokens, width), jnp.float32),
            jax.ShapeDtypeStruct((length - tokens, width), jnp.bfloat16),
            jax.ShapeDtypeStruct((2, width), jnp.float32),
        ],
        compiler_params=pltpu.CompilerParams(vmem_limit_bytes=24 * MIB),
        cost_estimate=pl.CostEstimate(flops=length * width, bytes_accessed=0, transcendentals=0),
        name="hidden_back",
    )(*values, weights, normed)


def attend_back_kernel(pieces, all_ref, lse_ref, *rest):
    grad_refs, (out_ref, key_acc, value_acc) = rest[:pieces], rest[pieces:]
    tokens = grad_refs[0].shape[0]
    scaling = HD**-0.5
    chunk = min(CHUNK, tokens)
    for head in range(2):
        base = head * 3 * HD
        _, keys, values = head_parts(all_ref, head)
        for at in range(0, pieces * tokens, chunk):
            span = slice(at, at + chunk)
            inner = slice(at % tokens, at % tokens + chunk)
            queries = head_parts(all_ref, head, span)[0]
            grads = grad_refs[at // tokens][inner, head * HD : (head + 1) * HD]
            lse = lse_ref[0, head : head + 1, span]
            probs = jnp.exp2(mm(keys, queries, NT) * SCALE2 - lse)
            product = probs * mm(values, grads, NT)
            inner_sum = jnp.sum(product, 0, keepdims=True)
            score_grad = (product - probs * inner_sum).astype(jnp.bfloat16)
            value_part = mm(probs.astype(jnp.bfloat16), grads)
            key_part = mm(score_grad, queries)
            if at == 0:
                value_acc[...] = value_part
                key_acc[...] = key_part
            else:
                value_acc[...] += value_part
                key_acc[...] += key_part
            query_grad = mm(keys, score_grad, TN) * scaling
            out_ref[span, base : base + HD] = query_grad.T.astype(jnp.bfloat16)
        out_ref[:, base + HD : base + 2 * HD] = (key_acc[...] * scaling).astype(jnp.bfloat16)
        out_ref[:, base + 2 * HD : base + 3 * HD] = value_acc[...].astype(jnp.bfloat16)


def attend_back(qkv, grad_pieces, lse, first, pairs):
    length = qkv.shape[0]
    columns = pairs * 6 * HD
    tokens = grad_pieces[0].shape[0]
    return pl.pallas_call(
        partial(attend_back_kernel, len(grad_pieces)),
        grid=(pairs,),
        in_specs=[
            pl.BlockSpec((length, 6 * HD), lambda p: (0, first + p)),
            pl.BlockSpec((1, 2, length), lambda p: (first + p, 0, 0)),
        ]
        + [pl.BlockSpec((tokens, 2 * HD), lambda p: (0, first + p))] * len(grad_pieces),
        out_specs=pl.BlockSpec((length, 6 * HD), lambda p: (0, p)),
        out_shape=jax.ShapeDtypeStruct((length, columns), jnp.bfloat16),
        scratch_shapes=[
            pltpu.VMEM((length, HD), jnp.float32),
            pltpu.VMEM((length, HD), jnp.float32),
        ],
        compiler_params=pltpu.CompilerParams(vmem_limit_bytes=32 * MIB),
        cost_estimate=pl.CostEstimate(
            flops=10 * pairs * 2 * HD * length * length,
            bytes_accessed=0,
            transcendentals=0,
        ),
        name="attend_back",
    )(qkv, lse, *grad_pieces)


def per_device(sizes, latents, cond, cotangent, w_qkv, w_out, w_up, w_down, w_ada, b_ada):
    shards, splits = sizes["fsdp"], sizes["seq"]
    me = lax.axis_index("seq")
    tokens, width = latents.shape[1:]
    heads = H // splits
    low = jnp.bfloat16
    wide = jnp.float32

    def fetch(value, step):
        return lax.ppermute(value, "seq", [((i + step) % splits, i) for i in range(splits)])

    def send(value, step):
        return lax.ppermute(value, "seq", [(i, (i + step) % splits) for i in range(splits)])

    def everyone(value):
        return [value] + [fetch(value, step) for step in range(1, splits)]

    def in_order(pieces, axis):
        if splits == 1:
            return pieces[0]
        return jnp.concatenate(
            [
                lax.select_n(
                    (position - me) % splits == 1, *pieces
                ) if splits == 2 else
                lax.dynamic_index_in_dim(
                    jnp.stack(pieces), (position - me) % splits, 0, keepdims=False
                )
                for position in range(splits)
            ],
            axis,
        )

    def seq_sum(value):
        if splits != 2:
            return lax.psum(value, "seq").astype(wide)
        return value.astype(wide) + fetch(value, 1).astype(wide)

    spot = lax.axis_index("fsdp")
    depth = shards // 4
    core_at, x_at, z_at = spot % 2, (spot // 2) % 2, spot // 4

    def core_swap(value):
        return lax.ppermute(value, "fsdp", [(i, i ^ 1) for i in range(shards)])

    def x_swap(value):
        return lax.ppermute(value, "fsdp", [(i, i ^ 2) for i in range(shards)])

    def z_send(value, step):
        return lax.ppermute(value, "fsdp", [(i, (i + 4 * step) % shards) for i in range(shards)])

    def two(mine, other, at):
        return jnp.stack(
            [jnp.where(at == 0, mine, other), jnp.where(at == 0, other, mine)], 1
        )

    def gather_z(shard):
        return [shard] + [z_send(shard, step) for step in range(1, depth)]

    def gather_x(pieces):
        rows, cols = pieces[0].shape
        line = jnp.zeros((depth, rows, cols), pieces[0].dtype)
        for step, piece in enumerate(pieces):
            line = lax.dynamic_update_slice_in_dim(line, piece[None], (z_at - step) % depth, 0)
        return line, x_swap(line)

    def gather_core(pair):
        rows, cols = pair[0].shape[1:]
        plane = two(*pair, x_at).reshape(2 * depth, rows, cols)
        return plane, core_swap(plane)

    def gather_end(pair):
        rows, cols = pair[0].shape[1:]
        return two(*pair, core_at).reshape(shards * rows, cols)

    blocks_at = jnp.arange(shards)
    place = (
        ((blocks_at % 2) ^ core_at) * 2 + ((blocks_at // 2) % 2 ^ x_at)
    ) * depth + (blocks_at // 4 - z_at) % depth
    place = place.astype(jnp.int32)

    def scatter_core(turned, value):
        half = turned.shape[0] // 2
        other = mm(turned[half:], value).astype(low)
        return mm(turned[:half], value).astype(low), core_swap(other)

    def x_part(pair):
        half = pair[0].shape[0] // 2
        return (pair[0][half:].astype(wide) + pair[1][half:].astype(wide)).astype(low)

    def scatter_x(pair, part):
        return *pair, x_swap(part)

    def scatter_z(*many):
        total = jnp.concatenate(
            [sum(part[: terms[2].shape[0]].astype(wide) for part in terms) for terms in many], 1
        )
        rows = total.shape[0] // depth
        return [total[:rows]] + [
            z_send(total[step * rows : (step + 1) * rows].astype(low), step)
            for step in range(1, depth)
        ]

    def tick(value):
        return core_swap(lax.slice(value, (0, 0), (16, 128)))

    def scatter_end(pieces):
        return sum(piece.astype(wide) for piece in pieces)

    after = lax.optimization_barrier
    own_latents, own_cotangent = latents[0], cotangent[0]
    cond_act, silu_back = jax.vjp(jax.nn.silu, cond.astype(wide))
    cond_all = lax.all_to_all(
        jnp.broadcast_to(cond_act.astype(low), (shards, width)),
        "fsdp",
        split_axis=0,
        concat_axis=0,
        tiled=True,
    )
    peer_latents = [fetch(own_latents, step) for step in range(1, splits)]
    cond_all, peer_latents = after((cond_all, peer_latents))
    mod_cols = (mm(cond_all, w_ada) + b_ada.astype(wide)).astype(low)
    modulation = lax.all_to_all(
        mod_cols, "fsdp", split_axis=0, concat_axis=1, tiled=True
    ).astype(wide)
    modulation, out_shard = after((modulation, w_out))
    out_pieces = gather_z(out_shard)
    shift_one, scale_one, gate_one, shift_two, scale_two, gate_two = [
        modulation[:, position * width : (position + 1) * width] for position in range(6)
    ]
    columns = heads * 3 * HD
    qkv_shard = lax.dynamic_slice_in_dim(w_qkv, me * columns, columns, 1)
    qkv_half = lax.all_gather(qkv_shard, "fsdp", axis=0, tiled=True)
    cond_all, up_shard, down_shard = after((cond_all, w_up, w_down))
    up_down = lax.all_gather(
        jnp.concatenate([up_shard, down_shard.T], 1), "fsdp", axis=0, tiled=True
    )
    units = w_up.shape[1]

    latents_all = jnp.concatenate([own_latents] + peer_latents, 0)
    cotangents = everyone(own_cotangent)

    normed_all, inverse_all = normalize(latents_all.astype(wide))
    hidden_one = (normed_all * (1.0 + scale_one) + shift_one).astype(low)
    qkv = mm(hidden_one, qkv_half).astype(low)
    qkv, out_pieces = after((qkv, out_pieces))
    out_pair = gather_x(out_pieces)
    attn_peers, lse_peers = attend(qkv, tokens, 1, splits - 1)
    attn_peers, qkv, cotangents = after((attn_peers, qkv, cotangents))
    blocks = [None] + [attn_peers[r * tokens : (r + 1) * tokens] for r in range(splits - 1)]
    theirs = [{} for _ in range(splits)]
    for r in range(1, splits):
        for q in range(1, splits):
            theirs[(r + q) % splits][q] = fetch(blocks[r], q)
    attn_own, lse_own = attend(qkv, tokens, 0, 1)
    blocks[0] = attn_own
    attn_own, out_pair, theirs = after((attn_own, out_pair, theirs))
    for q in range(1, splits):
        theirs[q][q] = fetch(attn_own, q)
    out_full = gather_end(gather_core(out_pair))

    def to_feed(rows, heads_of, piece):
        inputs = latents_all[piece * tokens : (piece + 1) * tokens].astype(wide)
        attn_rows = in_order([rows] + [heads_of[q] for q in range(1, splits)], 1)
        branch_one = mm(attn_rows, out_full)
        middle = inputs + gate_one * branch_one
        normed, inverse = normalize(middle)
        hidden = (normed * (1.0 + scale_two) + shift_two).astype(low)
        return hidden, attn_rows, branch_one, middle, normed, inverse

    own_theirs = theirs[0]
    hidden_two, attn_rows, branch_one, middle, normed_two, inverse_two = to_feed(
        attn_own, own_theirs, 0
    )
    hidden_two, theirs = after((hidden_two, theirs))
    grad_rows = (gate_two * jnp.concatenate(cotangents, 0).astype(wide)).astype(low)
    hidden_pieces = [hidden_two] + [
        to_feed(blocks[r], theirs[r], r)[0] for r in range(1, splits)
    ]

    hidden_all = jnp.concatenate(hidden_pieces, 0)
    turned_one, turned_two = turn(hidden_one, place), turn(hidden_all, place)
    turned_attn = turn(attn_rows, place)
    hidden_pieces, grad_rows, turned_one, turned_two, turned_attn = after(
        (hidden_pieces, grad_rows, turned_one, turned_two, turned_attn)
    )
    buffers, grad_parts, branch_parts = None, [None] * splits, [None] * splits
    grad_sent = []
    for piece in list(range(1, splits)) + [0]:
        act, grad_up, branch_parts[piece], grad_parts[piece] = feed(
            hidden_pieces[piece],
            grad_rows,
            up_down,
            piece,
            buffers,
            low if piece else wide,
        )
        buffers = (act, grad_up)
        if piece:
            grad_sent.append(send(grad_parts[piece], piece))
            beat, buffers = after((tick(grad_parts[piece]), buffers))

    def send_parts(parts):
        return [send(parts[step].astype(low), step) for step in range(1, splits)]

    def add_parts(own, received):
        for value in received:
            own = own + value.astype(wide)
        return own

    term_down = mm(grad_rows, act, TN).astype(low)
    term_down, grad_up = after((term_down, grad_up))
    grad_w_down = lax.psum_scatter(term_down, "fsdp", scatter_dimension=0, tiled=True)
    up_pair = scatter_core(turned_two, grad_up)
    up_part = x_part(up_pair)
    grad_sent, up_pair, up_part, branch_parts = after((grad_sent, up_pair, up_part, branch_parts))
    up_terms = scatter_x(up_pair, up_part)
    grad_hidden_two = add_parts(grad_parts[0], grad_sent)
    grad_mixed = own_cotangent.astype(wide)
    grad_shift_two = jnp.sum(grad_hidden_two, 0)
    grad_scale_two = jnp.sum(grad_hidden_two * normed_two, 0)
    grad_middle = grad_mixed + norm_grad(
        normed_two, inverse_two, grad_hidden_two * (1.0 + scale_two)
    )
    grad_gate_one = jnp.sum(grad_middle * branch_one, 0)
    grad_branch_one = (gate_one * grad_middle).astype(low)

    grad_attn = mm(grad_branch_one, out_full, NT).astype(low)
    own_width = heads * HD
    grad_pieces = [
        lax.dynamic_slice_in_dim(grad_attn, ((me + r) % splits) * own_width, own_width, 1)
        for r in range(splits)
    ]
    grad_arrived = [send(grad_pieces[r], r) for r in range(1, splits)]
    beat, turned_attn = after((tick(grad_pieces[-1]), turned_attn))
    out_pair = scatter_core(turned_attn, grad_branch_one)
    out_part = x_part(out_pair)
    grad_arrived, branch_parts, out_pair, out_part = after(
        (grad_arrived, branch_parts, out_pair, out_part)
    )
    branch_sent = send_parts(branch_parts)
    out_terms = scatter_x(out_pair, out_part)
    grad_heads = [grad_pieces[0]] + grad_arrived[::-1]
    lse = jnp.concatenate([lse_own, lse_peers], 2)
    pairs = heads // 2
    groups = 2 if pairs % 2 == 0 else 1
    each = pairs // groups
    size = each * 6 * HD
    values, first_terms = [], []
    for group in range(groups):
        value = attend_back(qkv, grad_heads, lse, group * each, each)
        values.append(value)
        if group + 1 < groups:
            values, up_terms = after((values, up_terms))
            pair = scatter_core(turned_one, values[0])
            up_pieces = scatter_z(up_terms)
            part = x_part(pair)
            pair, part, grad_heads, lse = after((pair, part, grad_heads, lse))
            first_terms = scatter_x(pair, part)
            beat, grad_heads = after((tick(part), grad_heads))
    values, first_terms, out_terms, branch_sent, grad_w_down = after(
        (values, first_terms, out_terms, branch_sent, grad_w_down)
    )
    pair = scatter_core(turned_one, values[-1])
    if groups == 1:
        up_pieces = scatter_z(up_terms)
    part = x_part(pair)
    pair, part, values, first_terms, out_terms = after(
        (pair, part, values, first_terms, out_terms)
    )
    last_terms = scatter_x(pair, part)
    beat, values = after((tick(part), values))
    joint_pieces = scatter_z(*([out_terms, first_terms] if groups > 1 else [out_terms]))
    own_grad, peers_grad, sums = hidden_back(values, qkv_half, normed_all, tokens)
    branch_two = add_parts(branch_parts[0], branch_sent)
    grad_gate_two = jnp.sum(grad_mixed * branch_two, 0)

    grad_mod_part = jnp.concatenate(
        [sums[0], sums[1], grad_gate_one, grad_shift_two, grad_scale_two, grad_gate_two]
    )[None]
    grad_mod = seq_sum(grad_mod_part).astype(low)
    hidden_parts = [own_grad] + [
        peers_grad[r * tokens : (r + 1) * tokens] for r in range(splits - 1)
    ]
    grad_mod, hidden_parts, last_terms = after((grad_mod, hidden_parts, last_terms))
    grad_mod_cols = lax.all_to_all(grad_mod, "fsdp", split_axis=1, concat_axis=0, tiled=True)
    hidden_sent = send_parts(hidden_parts)
    last_pieces = scatter_z(last_terms)
    mixed = (middle + gate_two * branch_two).astype(low)
    grad_w_ada = mm(cond_all, grad_mod_cols, TN)
    grad_b_ada = jnp.sum(grad_mod_cols.astype(wide), 0)
    cond_term = mm(grad_mod_cols, w_ada, NT).astype(low)
    cond_term, mixed, joint_pieces = after((cond_term, mixed, joint_pieces))
    cond_terms = lax.all_to_all(cond_term, "fsdp", split_axis=0, concat_axis=0, tiled=True)
    grad_w_up = scatter_end(up_pieces)
    grad_joint = scatter_end(joint_pieces).astype(low)
    grad_w_out = seq_sum(grad_joint[:, :width])
    grad_hidden_one = add_parts(hidden_parts[0], hidden_sent)
    grad_latents = grad_middle + norm_grad(
        normed_all[:tokens], inverse_all[:tokens], grad_hidden_one * (1.0 + scale_one)
    )
    grad_cond = silu_back(jnp.sum(cond_terms.astype(wide), 0, keepdims=True))[0]
    last_pieces, grad_latents, grad_cond, grad_w_out = after(
        (last_pieces, grad_latents, grad_cond, grad_w_out)
    )
    shards_qkv = [grad_joint[:, width:], scatter_end(last_pieces).astype(low)]
    grad_w_qkv = in_order(everyone(jnp.concatenate(shards_qkv, 1)), 1).astype(wide)
    return (
        mixed[None],
        grad_latents[None],
        grad_cond,
        grad_w_qkv,
        grad_w_out,
        grad_w_up,
        grad_w_down.T.astype(wide),
        grad_w_ada,
        grad_b_ada,
    )


def solution(mesh):
    return jax.shard_map(
        partial(per_device, dict(mesh.shape)),
        mesh=mesh,
        in_specs=(
            P("fsdp", "seq", None),
            P("fsdp", None),
            P("fsdp", "seq", None),
            P("fsdp", None),
            P("fsdp", None),
            P("fsdp", "seq"),
            P("seq", "fsdp"),
            P(None, "fsdp"),
            P("fsdp"),
        ),
        out_specs=(
            P("fsdp", "seq", None),
            P("fsdp", "seq", None),
            P("fsdp", None),
            P("fsdp", None),
            P("fsdp", None),
            P("fsdp", "seq"),
            P("seq", "fsdp"),
            P(None, "fsdp"),
            P("fsdp"),
        ),
        check_vma=False,
    )
```

profile of v0, /device:TPU:0, one launch (start us, length us, event | category | flops | bytes accessed | tf_op | source)
XLA Modules:
  0.0 397.4 jit_solution(17341571025989815116)
XLA Ops:
  14.2 12.4 %all_to_all.47 = bf16[16,2,512]{2,1,0:T(2,128)(2,1)S(1)} all-to-all(bf16[16,2,512]{2,1,0:T(2,128)(2,1)S(1)} %reshape.131), channel_id=1, replica_groups=mesh['fsdp'=16,'seq'=2] {'fsdp'}, dimensions={0} | all-to-all | bytes 65536 | tf_op jit(solution)/shard_map/all_to_all | solution.py:391
  26.7 8.8 %collective-permute-done = bf16[512,1024]{1,0:T(8,128)(2,1)S(1)} collective-permute-done((bf16[512,1024]{1,0:T(8,128)(2,1)}, bf16[512,1024]{1,0:T(8,128)(2,1)S(1)}, u32[]{:S(2)}, u32[]{:S(2)}) %collective-permute-start) | collective-permute-done | bytes 1048608 | tf_op jit(solution)/shard_map/ppermute | solution.py:288
  41.1 5.9 %all-to-all-start.1 = ((bf16[16,2,192]{2,1,0:T(2,128)(2,1)}), bf16[16,2,192]{2,1,0:T(2,128)(2,1)S(1)}, u32[]{:S(2)}, u32[]{:S(2)}) async-start(bf16[16,2,192]{2,1,0:T(2,128)(2,1)} %reshape.133), calls=%async_computation.1 | async-start | bytes 32768 | tf_op jit(solution)/shard_map/all_to_all | solution.py:401
  48.2 5.3 %all-to-all-done.1 = bf16[16,2,192]{2,1,0:T(2,128)(2,1)S(1)} async-done(((bf16[16,2,192]{2,1,0:T(2,128)(2,1)}), bf16[16,2,192]{2,1,0:T(2,128)(2,1)S(1)}, u32[]{:S(2)}, u32[]{:S(2)}) %all-to-all-start.1) | async-done | bytes 12320 | tf_op jit(solution)/shard_map/all_to_all | solution.py:401
  56.2 4.6 %fusion = (f32[1024,1024]{1,0:T(8,128)}, bf16[1024,1024]{1,0:T(8,128)(2,1)S(1)}) fusion(f32[1024]{0:T(1024)S(1)} %add_rsqrt_fusion, f32[1024]{0:T(1024)S(1)} %broadcast_multiply_fusion, bf16[512,1024]{1,0:T(8,128)(2,1)} %copy-done.38, bf16[512,1024]{1,0:T(8,128)(2,1)} %bitcast.82, f32[1024]{0:T(1024)S(1)} %bitcast.115, f32[1024]{0:T(1024)S(1)} %bitcast.103), kind=kLoop, calls=%fused_computation.2 | loop fusion | flops 9437184 | bytes 8404992 | tf_op jit(solution)/shard_map/mul | solution.py:32
  60.8 5.7 %convolution_convert_fusion.query_ref.all_ref = bf16[1024,1536]{1,0:T(8,128)(2,1)S(1)} fusion(bf16[1024,1024]{1,0:T(8,128)(2,1)S(1)} %get-tuple-element.254.value_ref, bf16[1024,1536]{1,0:T(8,128)(2,1)} %all-gather.3.cloned.1.call-done.refs_2_), kind=kOutput, calls=%fused_computation.7 | convolution fusion | flops 3222798336 | bytes 8388608 | tf_op jit(solution)/shard_map/dot_general | solution.py:26
  73.4 9.9 %attend.2 = (bf16[512,512]{1,0:T(8,128)(2,1)S(1)}, f32[4,2,512]{2,1,0:T(2,128)S(1)}) custom-call(bf16[1024,1536]{1,0:T(8,128)(2,1)S(1)} %convolution_convert_fusion.query_ref.all_ref, bf16[1024,1536]{1,0:T(8,128)(2,1)S(1)} %convolution_convert_fusion.query_ref.all_ref), custom_call_target="tpu_custom_call" | custom-call | flops 1073741824 | tf_op jit(solution)/shard_map/attend/pallas_call | solution.py:68
  86.9 9.9 %attend.3 = (bf16[512,512]{1,0:T(8,128)(2,1)S(1)}, f32[4,2,512]{2,1,0:T(2,128)S(1)}) custom-call(bf16[1024,1536]{1,0:T(8,128)(2,1)S(1)} %copy-done.2, bf16[1024,1536]{1,0:T(8,128)(2,1)S(1)} %copy-done.2), custom_call_target="tpu_custom_call" | custom-call | flops 1073741824 | tf_op jit(solution)/shard_map/attend/pallas_call | solution.py:68
  126.7 18.6 %all-gather.5.cloned.1.call-done.up_ref.down_ref = bf16[1024,4096]{1,0:T(8,128)(2,1)} async-done(((bf16[64,4096]{1,0:T(8,128)(2,1)}), bf16[1024,4096]{1,0:T(8,128)(2,1)}) %all-gather.5.cloned.1.call-update) | async-done | bytes 8388624 | tf_op jit(solution)/shard_map/all_gather | solution.py:413
  146.5 13.7 %feed.2 = (bf16[1024,2048]{1,0:T(8,128)(2,1)S(1)}, bf16[1024,2048]{1,0:T(8,128)(2,1)S(1)}, bf16[512,1024]{1,0:T(8,128)(2,1)S(1)}, bf16[512,1024]{1,0:T(8,128)(2,1)S(1)}) custom-call(bf16[512,1024]{1,0:T(8,128)(2,1)S(1)} %copy-done.9, bf16[1024,1024]{1,0:T(8,128)(2,1)S(1)} %multiply_convert_fusion.grad_ref, ...), custom_call_target="tpu_custom_call" | custom-call | flops 1073741824 | tf_op jit(solution)/shard_map/feed/pallas_call | solution.py:135
  162.2 14.9 %feed.3 = (bf16[1024,2048]{1,0:T(8,128)(2,1)S(1)}, bf16[1024,2048]{1,0:T(8,128)(2,1)}, f32[512,1024]{1,0:T(8,128)S(1)}, f32[512,1024]{1,0:T(8,128)S(1)}) custom-call(bf16[512,1024]{1,0:T(8,128)(2,1)S(1)} %copy-done.7, bf16[1024,1024]{1,0:T(8,128)(2,1)S(1)} %multiply_convert_fusion.grad_ref, ...), custom_call_target="tpu_custom_call", output_to_operand_aliasing={{0}: (4, {}), {1}: (5, {})} | custom-call | flops 1073741824 | tf_op jit(solution)/shard_map/feed/pallas_call | solution.py:135
  179.7 6.6 %convolution_convert_fusion.1 = bf16[1024,2048]{1,0:T(8,128)(2,1)} fusion(bf16[1024,1024]{1,0:T(8,128)(2,1)S(1)} %multiply_convert_fusion.grad_ref, bf16[1024,2048]{1,0:T(8,128)(2,1)S(1)} %get-tuple-element.158), kind=kOutput, calls=%fused_computation.8 | convolution fusion | flops 4297064448 | bytes 10485760 | tf_op jit(solution)/shard_map/dot_general | solution.py:26
  186.3 6.2 %convolution_convert_fusion.2 = bf16[512,2048]{1,0:T(8,128)(2,1)} fusion(bf16[1024,2048]{1,0:T(8,128)(2,1)} %get-tuple-element.160, bf16[1024,1024]{1,0:T(8,128)(2,1)} %copy-done.16), kind=kOutput, calls=%fused_computation.9 | convolution fusion | flops 2148532224 | bytes 7340032 | tf_op jit(solution)/shard_map/dot_general | solution.py:26
  194.3 4.8 %convolution_convert_fusion.3 = bf16[512,2048]{1,0:T(8,128)(2,1)S(1)} fusion(bf16[1024,2048]{1,0:T(8,128)(2,1)} %get-tuple-element.160, bf16[1024,1024]{1,0:T(8,128)(2,1)S(1)} %copy-done.17), kind=kOutput, calls=%fused_computation.10 | convolution fusion | flops 2148532224 | bytes 7340032 | tf_op jit(solution)/shard_map/dot_general | solution.py:26
  202.6 15.8 %collective-permute-done.9 = bf16[512,1024]{1,0:T(8,128)(2,1)S(1)} collective-permute-done((bf16[512,1024]{1,0:T(8,128)(2,1)}, bf16[512,1024]{1,0:T(8,128)(2,1)S(1)}, u32[]{:S(2)}, u32[]{:S(2)}) %collective-permute-start.9) | collective-permute-done | bytes 1048608 | tf_op jit(solution)/shard_map/ppermute | solution.py:291
  232.5 11.6 %collective-permute-done.11.rest_1_ = bf16[512,512]{1,0:T(8,128)(2,1)S(1)} collective-permute-done((bf16[512,512]{1,0:T(8,128)(2,1)S(1)}, bf16[512,512]{1,0:T(8,128)(2,1)S(1)}, u32[]{:S(2)}, u32[]{:S(2)}) %collective-permute-start.11) | collective-permute-done | bytes 524320 | tf_op jit(solution)/shard_map/ppermute | solution.py:291
  245.6 12.7 %attend_back.2.refs_0_ = bf16[1024,768]{1,0:T(8,128)(2,1)S(1)} custom-call(bf16[1024,1536]{1,0:T(8,128)(2,1)S(1)} %copy-done.3, f32[4,2,1024]{2,1,0:T(2,128)S(1)} %constant_dynamic-update-slice_fusion.lse_ref, bf16[512,512]{1,0:T(8,128)(2,1)S(1)} %get-tuple-element.175.rest_0_, bf16[512,512]{1,0:T(8,128)(2,1)S(1)} %collective-permute-done.11.rest_1_), custom_call_target="tpu_custom_call" | custom-call | flops 2684354560 | tf_op jit(solution)/shard_map/attend_back/pallas_call | solution.py:255
  269.0 5.5 %collective-permute-done.30 = bf16[64,2048]{1,0:T(8,128)(2,1)S(1)} collective-permute-done((bf16[64,2048]{1,0:T(8,128)(2,1)S(1)}, bf16[64,2048]{1,0:T(8,128)(2,1)S(1)}, u32[]{:S(2)}, u32[]{:S(2)}) %collective-permute-start.30) | collective-permute-done | bytes 262176 | tf_op jit(solution)/shard_map/ppermute | solution.py:328
  278.6 11.8 %collective-permute-done.31 = bf16[64,2048]{1,0:T(8,128)(2,1)S(1)} collective-permute-done((bf16[64,2048]{1,0:T(8,128)(2,1)S(1)}, bf16[64,2048]{1,0:T(8,128)(2,1)S(1)}, u32[]{:S(2)}, u32[]{:S(2)}) %collective-permute-start.31) | collective-permute-done | bytes 262176 | tf_op jit(solution)/shard_map/ppermute | solution.py:328
  291.3 12.8 %attend_back.3.refs_1_ = bf16[1024,768]{1,0:T(8,128)(2,1)S(1)} custom-call(bf16[1024,1536]{1,0:T(8,128)(2,1)S(1)} %copy-done.3, f32[4,2,1024]{2,1,0:T(2,128)S(1)} %constant_dynamic-update-slice_fusion.lse_ref, bf16[512,512]{1,0:T(8,128)(2,1)S(1)} %get-tuple-element.175.rest_0_, bf16[512,512]{1,0:T(8,128)(2,1)S(1)} %collective-permute-done.11.rest_1_), custom_call_target="tpu_custom_call" | custom-call | flops 2684354560 | tf_op jit(solution)/shard_map/attend_back/pallas_call | solution.py:255
  319.2 4.8 %hidden_back.1 = (f32[512,1024]{1,0:T(8,128)S(1)}, bf16[512,1024]{1,0:T(8,128)(2,1)S(1)}, f32[2,1024]{1,0:T(2,128)S(1)}) custom-call(bf16[1024,768]{1,0:T(8,128)(2,1)S(1)} %copy-done.21, bf16[1024,768]{1,0:T(8,128)(2,1)S(1)} %copy-done.23, bf16[1024,1536]{1,0:T(8,128)(2,1)S(1)} %copy-done.13, f32[1024,1024]{1,0:T(8,128)S(1)} %copy-done.4), custom_call_target="tpu_custom_call" | custom-call | flops 1048576 | tf_op jit(solution)/shard_map/hidden_back/pallas_call | solution.py:202
  330.8 6.8 %collective-permute-done.20 = bf16[256,768]{1,0:T(8,128)(2,1)} collective-permute-done((bf16[256,768]{1,0:T(8,128)(2,1)S(1)}, bf16[256,768]{1,0:T(8,128)(2,1)}, u32[]{:S(2)}, u32[]{:S(2)}) %collective-permute-start.20) | collective-permute-done | bytes 393248 | tf_op jit(solution)/shard_map/ppermute | solution.py:325
  361.4 4.6 %all-to-all-start.3 = ((bf16[16,2,512]{2,1,0:T(2,128)(2,1)}), bf16[16,2,512]{2,1,0:T(2,128)(2,1)S(1)}, u32[]{:S(2)}, u32[]{:S(2)}) async-start(bf16[16,2,512]{2,1,0:T(2,128)(2,1)} %reshape.137), calls=%async_computation.4 | async-start | bytes 65536 | tf_op jit(solution)/shard_map/all_to_all | solution.py:572
  368.1 4.6 %all-to-all-done.3 = bf16[16,2,512]{2,1,0:T(2,128)(2,1)S(1)} async-done(((bf16[16,2,512]{2,1,0:T(2,128)(2,1)}), bf16[16,2,512]{2,1,0:T(2,128)(2,1)S(1)}, u32[]{:S(2)}, u32[]{:S(2)}) %all-to-all-start.3) | async-done | bytes 32800 | tf_op jit(solution)/shard_map/all_to_all | solution.py:572
  (315 shorter events, 164.0 us)
Async XLA Ops:
  7.2 53.6 %all-gather.3.cloned.1.call-start = ((), (), s32[]{:S(2)}) async-start(), calls=%async_computation.5 | async-start | bytes 3342336 | tf_op jit(solution)/shard_map/all_gather | solution.py:411
  9.0 136.3 %all-gather.5.cloned.1.call-start = ((), (), s32[]{:S(2)}) async-start(), calls=%async_computation.6 | async-start | bytes 8912896 | tf_op jit(solution)/shard_map/all_gather | solution.py:413
  9.1 26.4 %collective-permute-start = (bf16[512,1024]{1,0:T(8,128)(2,1)}, bf16[512,1024]{1,0:T(8,128)(2,1)S(1)}, u32[]{:S(2)}, u32[]{:S(2)}) collective-permute-start(bf16[512,1024]{1,0:T(8,128)(2,1)} %bitcast.81), channel_id=1, source_target_pairs={{1,0},{0,1},{3,2},{2,3},{5,4},{4,5},{7,6},{6,7},{9,8},{8,9},{11,10... | collective-permute-start | bytes 3145736 | tf_op jit(solution)/shard_map/ppermute | solution.py:288
  37.7 45.6 %collective-permute-start.4 = (bf16[512,1024]{1,0:T(8,128)(2,1)}, bf16[512,1024]{1,0:T(8,128)(2,1)}, u32[]{:S(2)}, u32[]{:S(2)}) collective-permute-start(bf16[512,1024]{1,0:T(8,128)(2,1)} %bitcast.6), channel_id=1, source_target_pairs={{1,0},{0,1},{3,2},{2,3},{5,4},{4,5},{7,6},{6,7},{9,8},{8,9},{11,10... | collective-permute-start | bytes 3145736 | tf_op jit(solution)/shard_map/ppermute | solution.py:288
  47.0 259.3 %reduce-scatter.2.cloned.1.call-start = ((), (), s32[]{:S(2)}) async-start(), calls=%async_computation.7 | async-start | bytes 4456448 | tf_op jit(solution)/shard_map/reduce_scatter | solution.py:491
  54.2 15.1 %collective-permute-start.2 = (bf16[64,1024]{1,0:T(8,128)(2,1)S(1)}, bf16[64,1024]{1,0:T(8,128)(2,1)S(1)}, u32[]{:S(2)}, u32[]{:S(2)}) collective-permute-start(bf16[64,1024]{1,0:T(8,128)(2,1)S(1)} %copy-done.62), channel_id=1, source_target_pairs={{0,16},{2,18},{4,20},{6,22},{8,24},{10,26},{12,28},{14,30},{16,0},... | collective-permute-start | bytes 393224 | tf_op jit(solution)/shard_map/ppermute | solution.py:328
  55.6 13.7 %collective-permute-start.1 = (bf16[64,1024]{1,0:T(8,128)(2,1)S(1)}, bf16[64,1024]{1,0:T(8,128)(2,1)S(1)}, u32[]{:S(2)}, u32[]{:S(2)}) collective-permute-start(bf16[64,1024]{1,0:T(8,128)(2,1)S(1)} %copy-done.62), channel_id=1, source_target_pairs={{0,8},{2,10},{4,12},{6,14},{8,16},{10,18},{12,20},{14,22},{16,24},... | collective-permute-start | bytes 393224 | tf_op jit(solution)/shard_map/ppermute | solution.py:328
  72.8 24.0 %collective-permute-start.5 = (bf16[4,64,1024]{2,1,0:T(8,128)(2,1)}, bf16[4,64,1024]{2,1,0:T(8,128)(2,1)}, u32[]{:S(2)}, u32[]{:S(2)}) collective-permute-start(bf16[4,64,1024]{2,1,0:T(8,128)(2,1)} %bitcast_dynamic-update-slice_fusion), channel_id=1, source_target_pairs={{0,4},{2,6},{4,0},{6,2},{8,12},{10,14},{12,8},{14,10},{16,20},{18,... | collective-permute-start | bytes 1572872 | tf_op jit(solution)/shard_map/ppermute | solution.py:325
  105.3 14.6 %collective-permute-start.8 = (bf16[512,512]{1,0:T(8,128)(2,1)S(1)}, bf16[512,512]{1,0:T(8,128)(2,1)S(1)}, u32[]{:S(2)}, u32[]{:S(2)}) collective-permute-start(bf16[512,512]{1,0:T(8,128)(2,1)S(1)} %copy-done.27), channel_id=1, source_target_pairs={{1,0},{0,1},{3,2},{2,3},{5,4},{4,5},{7,6},{6,7},{9,8},{8,9},{11,10... | collective-permute-start | bytes 1572872 | tf_op jit(solution)/shard_map/ppermute | solution.py:288
  192.8 25.6 %collective-permute-start.9 = (bf16[512,1024]{1,0:T(8,128)(2,1)}, bf16[512,1024]{1,0:T(8,128)(2,1)S(1)}, u32[]{:S(2)}, u32[]{:S(2)}) collective-permute-start(bf16[512,1024]{1,0:T(8,128)(2,1)} %copy-done.31), channel_id=1, source_target_pairs={{0,1},{1,0},{2,3},{3,2},{4,5},{5,4},{6,7},{7,6},{8,9},{9,8},{10,11... | collective-permute-start | bytes 3145736 | tf_op jit(solution)/shard_map/ppermute | solution.py:291
  226.3 32.0 %collective-permute-start.13 = (bf16[256,2048]{1,0:T(8,128)(2,1)}, bf16[256,2048]{1,0:T(8,128)(2,1)S(1)}, u32[]{:S(2)}, u32[]{:S(2)}) collective-permute-start(bf16[256,2048]{1,0:T(8,128)(2,1)} %add_convert_fusion.2), channel_id=1, source_target_pairs={{0,4},{2,6},{4,0},{6,2},{8,12},{10,14},{12,8},{14,10},{16,20},{18,... | collective-permute-start | bytes 3145736 | tf_op jit(solution)/shard_map/ppermute | solution.py:325
  230.0 14.1 %collective-permute-start.11 = (bf16[512,512]{1,0:T(8,128)(2,1)S(1)}, bf16[512,512]{1,0:T(8,128)(2,1)S(1)}, u32[]{:S(2)}, u32[]{:S(2)}) collective-permute-start(bf16[512,512]{1,0:T(8,128)(2,1)S(1)} %get-tuple-element.260), channel_id=1, source_target_pairs={{0,1},{1,0},{2,3},{3,2},{4,5},{5,4},{6,7},{7,6},{8,9},{9,8},{10,11... | collective-permute-start | bytes 1572872 | tf_op jit(solution)/shard_map/ppermute | solution.py:291
  244.1 61.2 %collective-permute-start.17 = (bf16[512,1024]{1,0:T(8,128)(2,1)S(1)}, bf16[512,1024]{1,0:T(8,128)(2,1)S(1)}, u32[]{:S(2)}, u32[]{:S(2)}) collective-permute-start(bf16[512,1024]{1,0:T(8,128)(2,1)S(1)} %copy-done.29), channel_id=1, source_target_pairs={{0,1},{1,0},{2,3},{3,2},{4,5},{5,4},{6,7},{7,6},{8,9},{9,8},{10,11... | collective-permute-start | bytes 3145736 | tf_op jit(solution)/shard_map/ppermute | solution.py:291
  263.3 15.2 %collective-permute-start.32 = (bf16[64,2048]{1,0:T(8,128)(2,1)S(1)}, bf16[64,2048]{1,0:T(8,128)(2,1)S(1)}, u32[]{:S(2)}, u32[]{:S(2)}) collective-permute-start(bf16[64,2048]{1,0:T(8,128)(2,1)S(1)} %get-tuple-element.258), channel_id=1, source_target_pairs={{0,24},{2,26},{4,28},{6,30},{8,0},{10,2},{12,4},{14,6},{16,8},{18,... | collective-permute-start | bytes 786440 | tf_op jit(solution)/shard_map/ppermute | solution.py:328
  266.2 24.2 %collective-permute-start.31 = (bf16[64,2048]{1,0:T(8,128)(2,1)S(1)}, bf16[64,2048]{1,0:T(8,128)(2,1)S(1)}, u32[]{:S(2)}, u32[]{:S(2)}) collective-permute-start(bf16[64,2048]{1,0:T(8,128)(2,1)S(1)} %get-tuple-element.259), channel_id=1, source_target_pairs={{0,16},{2,18},{4,20},{6,22},{8,24},{10,26},{12,28},{14,30},{16,0},... | collective-permute-start | bytes 786440 | tf_op jit(solution)/shard_map/ppermute | solution.py:328
  267.2 38.1 %collective-permute-start.16 = (bf16[256,1024]{1,0:T(8,128)(2,1)S(1)}, bf16[256,1024]{1,0:T(8,128)(2,1)S(1)}, u32[]{:S(2)}, u32[]{:S(2)}) collective-permute-start(bf16[256,1024]{1,0:T(8,128)(2,1)S(1)} %add_convert_fusion.5), channel_id=1, source_target_pairs={{0,4},{2,6},{4,0},{6,2},{8,12},{10,14},{12,8},{14,10},{16,20},{18,... | collective-permute-start | bytes 1572872 | tf_op jit(solution)/shard_map/ppermute | solution.py:325
  274.5 31.8 %collective-permute-start.15 = (bf16[256,768]{1,0:T(8,128)(2,1)S(1)}, bf16[256,768]{1,0:T(8,128)(2,1)}, u32[]{:S(2)}, u32[]{:S(2)}) collective-permute-start(bf16[256,768]{1,0:T(8,128)(2,1)S(1)} %add_convert_fusion.7), channel_id=1, source_target_pairs={{0,4},{2,6},{4,0},{6,2},{8,12},{10,14},{12,8},{14,10},{16,20},{18,... | collective-permute-start | bytes 1179656 | tf_op jit(solution)/shard_map/ppermute | solution.py:325
  328.4 24.2 %collective-permute-start.23 = (bf16[64,1792]{1,0:T(8,128)(2,1)}, bf16[64,1792]{1,0:T(8,128)(2,1)}, u32[]{:S(2)}, u32[]{:S(2)}) collective-permute-start(bf16[64,1792]{1,0:T(8,128)(2,1)} %get-tuple-element.268), channel_id=1, source_target_pairs={{0,24},{2,26},{4,28},{6,30},{8,0},{10,2},{12,4},{14,6},{16,8},{18,... | collective-permute-start | bytes 688136 | tf_op jit(solution)/shard_map/ppermute | solution.py:328
  330.2 25.8 %collective-permute-start.22 = (bf16[64,1792]{1,0:T(8,128)(2,1)}, bf16[64,1792]{1,0:T(8,128)(2,1)}, u32[]{:S(2)}, u32[]{:S(2)}) collective-permute-start(bf16[64,1792]{1,0:T(8,128)(2,1)} %get-tuple-element.269), channel_id=1, source_target_pairs={{0,16},{2,18},{4,20},{6,22},{8,24},{10,26},{12,28},{14,30},{16,0},... | collective-permute-start | bytes 688136 | tf_op jit(solution)/shard_map/ppermute | solution.py:328
  330.2 27.2 %collective-permute-start.21 = (bf16[64,1792]{1,0:T(8,128)(2,1)}, bf16[64,1792]{1,0:T(8,128)(2,1)}, u32[]{:S(2)}, u32[]{:S(2)}) collective-permute-start(bf16[64,1792]{1,0:T(8,128)(2,1)} %get-tuple-element.270), channel_id=1, source_target_pairs={{0,8},{2,10},{4,12},{6,14},{8,16},{10,18},{12,20},{14,22},{16,24},... | collective-permute-start | bytes 688136 | tf_op jit(solution)/shard_map/ppermute | solution.py:328
  343.0 32.0 %collective-permute-start.27 = (bf16[512,1024]{1,0:T(8,128)(2,1)}, bf16[512,1024]{1,0:T(8,128)(2,1)}, u32[]{:S(2)}, u32[]{:S(2)}) collective-permute-start(bf16[512,1024]{1,0:T(8,128)(2,1)} %copy-done.30), channel_id=1, source_target_pairs={{0,1},{1,0},{2,3},{3,2},{4,5},{5,4},{6,7},{7,6},{8,9},{9,8},{10,11... | collective-permute-start | bytes 3145736 | tf_op jit(solution)/shard_map/ppermute | solution.py:291
  345.9 36.1 %collective-permute-start.26 = (bf16[64,768]{1,0:T(8,128)(2,1)}, bf16[64,768]{1,0:T(8,128)(2,1)}, u32[]{:S(2)}, u32[]{:S(2)}) collective-permute-start(bf16[64,768]{1,0:T(8,128)(2,1)} %get-tuple-element.273), channel_id=1, source_target_pairs={{0,24},{2,26},{4,28},{6,30},{8,0},{10,2},{12,4},{14,6},{16,8},{18,... | collective-permute-start | bytes 294920 | tf_op jit(solution)/shard_map/ppermute | solution.py:328
  352.6 29.4 %collective-permute-start.25 = (bf16[64,768]{1,0:T(8,128)(2,1)}, bf16[64,768]{1,0:T(8,128)(2,1)}, u32[]{:S(2)}, u32[]{:S(2)}) collective-permute-start(bf16[64,768]{1,0:T(8,128)(2,1)} %get-tuple-element.274), channel_id=1, source_target_pairs={{0,16},{2,18},{4,20},{6,22},{8,24},{10,26},{12,28},{14,30},{16,0},... | collective-permute-start | bytes 294920 | tf_op jit(solution)/shard_map/ppermute | solution.py:328
  355.9 26.0 %collective-permute-start.24 = (bf16[64,768]{1,0:T(8,128)(2,1)}, bf16[64,768]{1,0:T(8,128)(2,1)}, u32[]{:S(2)}, u32[]{:S(2)}) collective-permute-start(bf16[64,768]{1,0:T(8,128)(2,1)} %get-tuple-element.275), channel_id=1, source_target_pairs={{0,8},{2,10},{4,12},{6,14},{8,16},{10,18},{12,20},{14,22},{16,24},... | collective-permute-start | bytes 294920 | tf_op jit(solution)/shard_map/ppermute | solution.py:328
  (82 other events, 865.8 us)
Sparse Core Ops, SparseCore 0:
  10.9 48.9 all-gather.2
  62.6 82.6 all-gather.4
  192.9 82.7 reduce-scatter.1
where the time goes:
time: 402 us; the launch traced here: 397 us
  waiting for transfers between devices  101 us (25%)
  Pallas kernels  84.7 us (21%)
  starting transfers between devices  53.4 us (13%)
  other arithmetic  53.2 us (13%)
  matrix products  41.7 us (10%)
  local copies, waits for them, and re-layouts  36.3 us (9%)
  between operations  15.2 us (4%)
  blocking collectives  12.4 us (3%)
    dot_general x16, matrix products, mm(): return lax.dot_general(a, b, dims, preferred_element_type=jnp.float32)  41.7 us
    pallas_call x2, Pallas kernels, feed(): pl.pallas_call(partial(feed_kernel, int(aliased)), grid=(count,), in_spec...  28.6 us
    unnamed x147, local copies, waits for them, and re-layouts  28.5 us
    ppermute x4, waiting for transfers between devices, send(): lax.ppermute(value, 'seq', [(i, (i + step) % splits) for i in range(split...  27.4 us
    pallas_call x2, Pallas kernels, attend_back(): pl.pallas_call(partial(attend_back_kernel, len(grad_pieces)), grid=(pairs...  25.5 us
    ppermute x12, waiting for transfers between devices, z_send(): lax.ppermute(value, 'fsdp', [(i, (i + 4 * step) % shards) for i in range(...  22.6 us
    pallas_call x2, Pallas kernels, attend(): pl.pallas_call(attend_kernel, grid=(pairs, count), in_specs=[pl.BlockSpec...  19.9 us
    all_gather x1, waiting for transfers between devices, per_device(): lax.all_gather(jnp.concatenate([up_shard, down_shard.T], 1), 'fsdp', axis...  18.6 us
  transfers between devices with their start and end apart: 39, of which 15 were waited for; matrix products, arithmetic and copies ran while one was open for 22% of the time, Pallas kernels for 13%

commit v1 on v0

--- a/solution.py
+++ b/solution.py
@@ -82,7 +82,7 @@
         ],
         compiler_params=pltpu.CompilerParams(vmem_limit_bytes=24 * MIB),
         cost_estimate=pl.CostEstimate(
-            flops=4 * pairs * 2 * HD * length * count * tokens,
+            flops=pairs * length * count * tokens,
             bytes_accessed=0,
             transcendentals=0,
         ),
@@ -149,7 +149,7 @@
         input_output_aliases={4: 0, 5: 1} if aliased else {},
         compiler_params=pltpu.CompilerParams(vmem_limit_bytes=40 * MIB),
         cost_estimate=pl.CostEstimate(
-            flops=tokens * width * units, bytes_accessed=0, transcendentals=0
+            flops=tokens * units, bytes_accessed=0, transcendentals=0
         ),
         name="feed",
     )(hidden, grads_all, up_down, up_down, *(buffers or ()))
@@ -211,7 +211,9 @@
             jax.ShapeDtypeStruct((2, width), jnp.float32),
         ],
         compiler_params=pltpu.CompilerParams(vmem_limit_bytes=24 * MIB),
-        cost_estimate=pl.CostEstimate(flops=length * width, bytes_accessed=0, transcendentals=0),
+        cost_estimate=pl.CostEstimate(
+            flops=length * width, bytes_accessed=0, transcendentals=0
+        ),
         name="hidden_back",
     )(*values, weights, normed)
 
@@ -268,7 +270,7 @@
         ],
         compiler_params=pltpu.CompilerParams(vmem_limit_bytes=32 * MIB),
         cost_estimate=pl.CostEstimate(
-            flops=10 * pairs * 2 * HD * length * length,
+            flops=pairs * length * length,
             bytes_accessed=0,
             transcendentals=0,
         ),
@@ -378,9 +380,6 @@
             z_send(total[step * rows : (step + 1) * rows].astype(low), step)
             for step in range(1, depth)
         ]
-
-    def tick(value):
-        return core_swap(lax.slice(value, (0, 0), (16, 128)))
 
     def scatter_end(pieces):
         return sum(piece.astype(wide) for piece in pieces)
@@ -476,7 +475,6 @@
         buffers = (act, grad_up)
         if piece:
             grad_sent.append(send(grad_parts[piece], piece))
-            beat, buffers = after((tick(grad_parts[piece]), buffers))
 
     def send_parts(parts):
         return [send(parts[step].astype(low), step) for step in range(1, splits)]
@@ -486,13 +484,7 @@
             own = own + value.astype(wide)
         return own
 
-    term_down = mm(grad_rows, act, TN).astype(low)
-    term_down, grad_up = after((term_down, grad_up))
-    grad_w_down = lax.psum_scatter(term_down, "fsdp", scatter_dimension=0, tiled=True)
-    up_pair = scatter_core(turned_two, grad_up)
-    up_part = x_part(up_pair)
-    grad_sent, up_pair, up_part, branch_parts = after((grad_sent, up_pair, up_part, branch_parts))
-    up_terms = scatter_x(up_pair, up_part)
+    grad_sent, act, grad_up, branch_parts = after((grad_sent, act, grad_up, branch_parts))
     grad_hidden_two = add_parts(grad_parts[0], grad_sent)
     grad_mixed = own_cotangent.astype(wide)
     grad_shift_two = jnp.sum(grad_hidden_two, 0)
@@ -510,12 +502,18 @@
         for r in range(splits)
     ]
     grad_arrived = [send(grad_pieces[r], r) for r in range(1, splits)]
-    beat, turned_attn = after((tick(grad_pieces[-1]), turned_attn))
+    term_down = mm(grad_rows, act, TN).astype(low)
+    grad_arrived, branch_parts, term_down, act, grad_up = after(
+        (grad_arrived, branch_parts, term_down, act, grad_up)
+    )
+    grad_w_down = lax.psum_scatter(term_down, "fsdp", scatter_dimension=0, tiled=True)
+    up_pair = scatter_core(turned_two, grad_up)
     out_pair = scatter_core(turned_attn, grad_branch_one)
-    out_part = x_part(out_pair)
-    grad_arrived, branch_parts, out_pair, out_part = after(
-        (grad_arrived, branch_parts, out_pair, out_part)
-    )
+    up_part, out_part = x_part(up_pair), x_part(out_pair)
+    up_pair, out_pair, up_part, out_part, grad_arrived = after(
+        (up_pair, out_pair, up_part, out_part, grad_arrived)
+    )
+    up_terms = scatter_x(up_pair, up_part)
     branch_sent = send_parts(branch_parts)
     out_terms = scatter_x(out_pair, out_part)
     grad_heads = [grad_pieces[0]] + grad_arrived[::-1]
@@ -535,21 +533,20 @@
             part = x_part(pair)
             pair, part, grad_heads, lse = after((pair, part, grad_heads, lse))
             first_terms = scatter_x(pair, part)
-            beat, grad_heads = after((tick(part), grad_heads))
-    values, first_terms, out_terms, branch_sent, grad_w_down = after(
-        (values, first_terms, out_terms, branch_sent, grad_w_down)
-    )
-    pair = scatter_core(turned_one, values[-1])
     if groups == 1:
         up_pieces = scatter_z(up_terms)
+    values, first_terms, out_terms, up_pieces, branch_sent, grad_w_down = after(
+        (values, first_terms, out_terms, up_pieces, branch_sent, grad_w_down)
+    )
+    pair = scatter_core(turned_one, values[-1])
     part = x_part(pair)
-    pair, part, values, first_terms, out_terms = after(
-        (pair, part, values, first_terms, out_terms)
-    )
+    pair, part, values = after((pair, part, values))
     last_terms = scatter_x(pair, part)
-    beat, values = after((tick(part), values))
+    own_grad, peers_grad, sums = hidden_back(values, qkv_half, normed_all, tokens)
+    own_grad, peers_grad, sums, first_terms, out_terms = after(
+        (own_grad, peers_grad, sums, first_terms, out_terms)
+    )
     joint_pieces = scatter_z(*([out_terms, first_terms] if groups > 1 else [out_terms]))
-    own_grad, peers_grad, sums = hidden_back(values, qkv_half, normed_all, tokens)
     branch_two = add_parts(branch_parts[0], branch_sent)
     grad_gate_two = jnp.sum(grad_mixed * branch_two, 0)
 
@@ -560,15 +557,18 @@
     hidden_parts = [own_grad] + [
         peers_grad[r * tokens : (r + 1) * tokens] for r in range(splits - 1)
     ]
-    grad_mod, hidden_parts, last_terms = after((grad_mod, hidden_parts, last_terms))
+    grad_mod, hidden_parts = after((grad_mod, hidden_parts))
     grad_mod_cols = lax.all_to_all(grad_mod, "fsdp", split_axis=1, concat_axis=0, tiled=True)
     hidden_sent = send_parts(hidden_parts)
+    grad_mod_cols, last_terms, up_pieces, grad_w_down = after(
+        (grad_mod_cols, last_terms, up_pieces, grad_w_down)
+    )
     last_pieces = scatter_z(last_terms)
-    mixed = (middle + gate_two * branch_two).astype(low)
     grad_w_ada = mm(cond_all, grad_mod_cols, TN)
     grad_b_ada = jnp.sum(grad_mod_cols.astype(wide), 0)
     cond_term = mm(grad_mod_cols, w_ada, NT).astype(low)
-    cond_term, mixed, joint_pieces = after((cond_term, mixed, joint_pieces))
+    cond_term, middle, joint_pieces = after((cond_term, middle, joint_pieces))
+    mixed = (middle + gate_two * branch_two).astype(low)
     cond_terms = lax.all_to_all(cond_term, "fsdp", split_axis=0, concat_axis=0, tiled=True)
     grad_w_up = scatter_end(up_pieces)
     grad_joint = scatter_end(joint_pieces).astype(low)

time: 402 us -> 419 us (1.042)
  waiting for transfers between devices: 101 us -> 116 us
  matrix products: 41.7 us -> 34.3 us
  local copies, waits for them, and re-layouts: 36.3 us -> 42.1 us
    reduce_scatter x1, waiting for transfers between devices: 0.01 us -> 15.7 us  [per_device(): lax.psum_scatter(term_down, 'fsdp', scatter_dimension=0, tiled=True)]
    ppermute x4, waiting for transfers between devices: 27.4 us -> 12.3 us  [send(): lax.ppermute(value, 'seq', [(i, (i + step) % splits) for i in range(split...]
    ppermute x12, waiting for transfers between devices: 22.6 us -> 33.7 us  [z_send(): lax.ppermute(value, 'fsdp', [(i, (i + 4 * step) % shards) for i in range(...]
    ppermute x5, waiting for transfers between devices: 6.82 us -> 14.4 us  [x_swap(): return lax.ppermute(value, 'fsdp', [(i, i ^ 2) for i in range(shards)])]
    dot_general x16, matrix products: 41.7 us -> 34.3 us  [mm(): return lax.dot_general(a, b, dims, preferred_element_type=jnp.float32)]
    all_to_all x1, waiting for transfers between devices: 4.58 us -> 0.16 us  [per_device(): lax.all_to_all(cond_term, 'fsdp', split_axis=0, concat_axis=0, tiled=True)]
    unnamed x147 -> x170, local copies, waits for them, and re-layouts: 28.5 us -> 31.4 us
  transfers between devices with their start and end apart: 39 -> 39, of which waited for: 15 -> 18; matrix products, arithmetic and copies ran while one was open for 22% -> 22% of each run, Pallas kernels for 13% -> 16%
where the time goes in v1:
time: 419 us; the launch traced here: 415 us
  waiting for transfers between devices  116 us (28%)
  Pallas kernels  87.1 us (21%)
  other arithmetic  56.5 us (13%)
  starting transfers between devices  50.6 us (12%)
  local copies, waits for them, and re-layouts  42.1 us (10%)
  matrix products  34.3 us (8%)
  between operations  15.3 us (4%)
  blocking collectives  12.4 us (3%)
    dot_general x16, matrix products, mm(): return lax.dot_general(a, b, dims, preferred_element_type=jnp.float32)  34.3 us
    ppermute x12, waiting for transfers between devices, z_send(): lax.ppermute(value, 'fsdp', [(i, (i + 4 * step) % shards) for i in range(...  33.7 us
    unnamed x170, local copies, waits for them, and re-layouts  31.4 us
    pallas_call x2, Pallas kernels, feed(): pl.pallas_call(partial(feed_kernel, int(aliased)), grid=(count,), in_spec...  29 us
    pallas_call x2, Pallas kernels, attend_back(): pl.pallas_call(partial(attend_back_kernel, len(grad_pieces)), grid=(pairs...  27 us
    pallas_call x2, Pallas kernels, attend(): pl.pallas_call(attend_kernel, grid=(pairs, count), in_specs=[pl.BlockSpec...  19.9 us
    all_gather x1, waiting for transfers between devices, per_device(): lax.all_gather(jnp.concatenate([up_shard, down_shard.T], 1), 'fsdp', axis...  18.5 us
    reduce_scatter x1, waiting for transfers between devices, per_device(): lax.psum_scatter(term_down, 'fsdp', scatter_dimension=0, tiled=True)  15.7 us
  transfers between devices with their start and end apart: 39, of which 18 were waited for; matrix products, arithmetic and copies ran while one was open for 22% of the time, Pallas kernels for 16%

profile of v1, /device:TPU:0, one launch (start us, length us, event | category | flops | bytes accessed | tf_op | source)
XLA Modules:
  0.0 414.5 jit_solution(16204290284659751654)
XLA Ops:
  14.8 12.4 %all_to_all.47 = bf16[16,2,512]{2,1,0:T(2,128)(2,1)S(1)} all-to-all(bf16[16,2,512]{2,1,0:T(2,128)(2,1)S(1)} %reshape.131), channel_id=1, replica_groups=mesh['fsdp'=16,'seq'=2] {'fsdp'}, dimensions={0} | all-to-all | bytes 65536 | tf_op jit(solution)/shard_map/all_to_all | solution.py:390
  27.3 8.2 %collective-permute-done = bf16[512,1024]{1,0:T(8,128)(2,1)S(1)} collective-permute-done((bf16[512,1024]{1,0:T(8,128)(2,1)}, bf16[512,1024]{1,0:T(8,128)(2,1)S(1)}, u32[]{:S(2)}, u32[]{:S(2)}) %collective-permute-start) | collective-permute-done | bytes 1048608 | tf_op jit(solution)/shard_map/ppermute | solution.py:290
  41.1 5.9 %all-to-all-start.1 = ((bf16[16,2,192]{2,1,0:T(2,128)(2,1)}), bf16[16,2,192]{2,1,0:T(2,128)(2,1)S(1)}, u32[]{:S(2)}, u32[]{:S(2)}) async-start(bf16[16,2,192]{2,1,0:T(2,128)(2,1)} %reshape.133), calls=%async_computation.1 | async-start | bytes 32768 | tf_op jit(solution)/shard_map/all_to_all | solution.py:400
  48.2 5.3 %all-to-all-done.1 = bf16[16,2,192]{2,1,0:T(2,128)(2,1)S(1)} async-done(((bf16[16,2,192]{2,1,0:T(2,128)(2,1)}), bf16[16,2,192]{2,1,0:T(2,128)(2,1)S(1)}, u32[]{:S(2)}, u32[]{:S(2)}) %all-to-all-start.1) | async-done | bytes 12320 | tf_op jit(solution)/shard_map/all_to_all | solution.py:400
  56.2 4.6 %fusion = (f32[1024,1024]{1,0:T(8,128)}, bf16[1024,1024]{1,0:T(8,128)(2,1)S(1)}) fusion(f32[1024]{0:T(1024)S(1)} %add_rsqrt_fusion, f32[1024]{0:T(1024)S(1)} %broadcast_multiply_fusion, bf16[512,1024]{1,0:T(8,128)(2,1)} %copy-done.39, bf16[512,1024]{1,0:T(8,128)(2,1)} %bitcast.82, f32[1024]{0:T(1024)S(1)} %bitcast.115, f32[1024]{0:T(1024)S(1)} %bitcast.103), kind=kLoop, calls=%fused_computation.2 | loop fusion | flops 9437184 | bytes 8404992 | tf_op jit(solution)/shard_map/mul | solution.py:32
  60.8 5.7 %convolution_convert_fusion.query_ref.all_ref = bf16[1024,1536]{1,0:T(8,128)(2,1)S(1)} fusion(bf16[1024,1024]{1,0:T(8,128)(2,1)S(1)} %get-tuple-element.272.value_ref, bf16[1024,1536]{1,0:T(8,128)(2,1)} %all-gather.3.cloned.1.call-done.refs_2_), kind=kOutput, calls=%fused_computation.7 | convolution fusion | flops 3222798336 | bytes 8388608 | tf_op jit(solution)/shard_map/dot_general | solution.py:26
  73.4 9.9 %attend.2 = (bf16[512,512]{1,0:T(8,128)(2,1)S(1)}, f32[4,2,512]{2,1,0:T(2,128)S(1)}) custom-call(bf16[1024,1536]{1,0:T(8,128)(2,1)S(1)} %convolution_convert_fusion.query_ref.all_ref, bf16[1024,1536]{1,0:T(8,128)(2,1)S(1)} %convolution_convert_fusion.query_ref.all_ref), custom_call_target="tpu_custom_call" | custom-call | flops 2097152 | tf_op jit(solution)/shard_map/attend/pallas_call | solution.py:68
  86.9 9.9 %attend.3 = (bf16[512,512]{1,0:T(8,128)(2,1)S(1)}, f32[4,2,512]{2,1,0:T(2,128)S(1)}) custom-call(bf16[1024,1536]{1,0:T(8,128)(2,1)S(1)} %copy-done.2, bf16[1024,1536]{1,0:T(8,128)(2,1)S(1)} %copy-done.2), custom_call_target="tpu_custom_call" | custom-call | flops 2097152 | tf_op jit(solution)/shard_map/attend/pallas_call | solution.py:68
  126.8 18.5 %all-gather.5.cloned.1.call-done.up_ref.down_ref = bf16[1024,4096]{1,0:T(8,128)(2,1)} async-done(((bf16[64,4096]{1,0:T(8,128)(2,1)}), bf16[1024,4096]{1,0:T(8,128)(2,1)}) %all-gather.5.cloned.1.call-update) | async-done | bytes 8388624 | tf_op jit(solution)/shard_map/all_gather | solution.py:412
  146.5 14.7 %feed.2 = (bf16[1024,2048]{1,0:T(8,128)(2,1)S(1)}, bf16[1024,2048]{1,0:T(8,128)(2,1)S(1)}, bf16[512,1024]{1,0:T(8,128)(2,1)S(1)}, bf16[512,1024]{1,0:T(8,128)(2,1)}) custom-call(bf16[512,1024]{1,0:T(8,128)(2,1)S(1)} %copy-done.9, bf16[1024,1024]{1,0:T(8,128)(2,1)S(1)} %multiply_convert_fusion.grad_ref, ...), custom_call_target="tpu_custom_call" | custom-call | flops 1048576 | tf_op jit(solution)/shard_map/feed/pallas_call | solution.py:135
  171.1 14.3 %feed.3 = (bf16[1024,2048]{1,0:T(8,128)(2,1)S(1)}, bf16[1024,2048]{1,0:T(8,128)(2,1)}, f32[512,1024]{1,0:T(8,128)S(1)}, f32[512,1024]{1,0:T(8,128)S(1)}) custom-call(bf16[512,1024]{1,0:T(8,128)(2,1)S(1)} %copy-done.7, bf16[1024,1024]{1,0:T(8,128)(2,1)S(1)} %multiply_convert_fusion.grad_ref, ...), custom_call_target="tpu_custom_call", output_to_operand_aliasing={{0}: (4, {}), {1}: (5, {})} | custom-call | flops 1048576 | tf_op jit(solution)/shard_map/feed/pallas_call | solution.py:135
  185.3 6.5 %collective-permute-done.9 = bf16[512,1024]{1,0:T(8,128)(2,1)} collective-permute-done((bf16[512,1024]{1,0:T(8,128)(2,1)}, bf16[512,1024]{1,0:T(8,128)(2,1)}, u32[]{:S(2)}, u32[]{:S(2)}) %collective-permute-start.9) | collective-permute-done | bytes 1048608 | tf_op jit(solution)/shard_map/ppermute | solution.py:293
  202.8 6.3 %convolution_convert_fusion.1 = bf16[1024,2048]{1,0:T(8,128)(2,1)} fusion(bf16[1024,1024]{1,0:T(8,128)(2,1)S(1)} %multiply_convert_fusion.grad_ref, bf16[1024,2048]{1,0:T(8,128)(2,1)S(1)} %get-tuple-element.173), kind=kOutput, calls=%fused_computation.8 | convolution fusion | flops 4297064448 | bytes 10485760 | tf_op jit(solution)/shard_map/dot_general | solution.py:26
  209.1 5.8 %collective-permute-done.10.rest_1_ = bf16[512,512]{1,0:T(8,128)(2,1)} collective-permute-done((bf16[512,512]{1,0:T(8,128)(2,1)}, bf16[512,512]{1,0:T(8,128)(2,1)}, u32[]{:S(2)}, u32[]{:S(2)}) %collective-permute-start.10) | collective-permute-done | bytes 524320 | tf_op jit(solution)/shard_map/ppermute | solution.py:293
  214.9 4.7 %convolution_convert_fusion.2 = bf16[512,2048]{1,0:T(8,128)(2,1)S(1)} fusion(bf16[1024,2048]{1,0:T(8,128)(2,1)} %get-tuple-element.175, bf16[1024,1024]{1,0:T(8,128)(2,1)S(1)} %copy-done.26), kind=kOutput, calls=%fused_computation.9 | convolution fusion | flops 2148532224 | bytes 7340032 | tf_op jit(solution)/shard_map/dot_general | solution.py:26
  230.4 13.5 %attend_back.2.refs_0_ = bf16[1024,768]{1,0:T(8,128)(2,1)S(1)} custom-call(bf16[1024,1536]{1,0:T(8,128)(2,1)S(1)} %copy-done.3, f32[4,2,1024]{2,1,0:T(2,128)S(1)} %constant_dynamic-update-slice_fusion.lse_ref, bf16[512,512]{1,0:T(8,128)(2,1)S(1)} %get-tuple-element.184.rest_0_, bf16[512,512]{1,0:T(8,128)(2,1)} %collective-permute-done.10.rest_1_), custom_call_target="tpu_custom_call" | custom-call | flops 2097152 | tf_op jit(solution)/shard_map/attend_back/pallas_call | solution.py:257
  243.9 14.4 %collective-permute-done.13 = bf16[256,2048]{1,0:T(8,128)(2,1)S(1)} collective-permute-done((bf16[256,2048]{1,0:T(8,128)(2,1)S(1)}, bf16[256,2048]{1,0:T(8,128)(2,1)S(1)}, u32[]{:S(2)}, u32[]{:S(2)}) %collective-permute-start.13) | collective-permute-done | bytes 1048608 | tf_op jit(solution)/shard_map/ppermute | solution.py:327
  266.0 13.5 %attend_back.3.refs_1_ = bf16[1024,768]{1,0:T(8,128)(2,1)S(1)} custom-call(bf16[1024,1536]{1,0:T(8,128)(2,1)S(1)} %copy-done.3, f32[4,2,1024]{2,1,0:T(2,128)S(1)} %constant_dynamic-update-slice_fusion.lse_ref, bf16[512,512]{1,0:T(8,128)(2,1)S(1)} %get-tuple-element.184.rest_0_, bf16[512,512]{1,0:T(8,128)(2,1)} %collective-permute-done.10.rest_1_), custom_call_target="tpu_custom_call" | custom-call | flops 2097152 | tf_op jit(solution)/shard_map/attend_back/pallas_call | solution.py:257
  282.3 13.3 %collective-permute-done.18 = bf16[64,2048]{1,0:T(8,128)(2,1)S(1)} collective-permute-done((bf16[64,2048]{1,0:T(8,128)(2,1)S(1)}, bf16[64,2048]{1,0:T(8,128)(2,1)S(1)}, u32[]{:S(2)}, u32[]{:S(2)}) %collective-permute-start.18) | collective-permute-done | bytes 262176 | tf_op jit(solution)/shard_map/ppermute | solution.py:330
  297.1 15.7 %reduce-scatter.2.cloned.1.call-done = bf16[64,2048]{1,0:T(8,128)(2,1)} async-done(((bf16[1024,2048]{1,0:T(8,128)(2,1)}), bf16[64,2048]{1,0:T(8,128)(2,1)}) %reduce-scatter.2.cloned.1.call-update) | async-done | bytes 262160 | tf_op jit(solution)/shard_map/reduce_scatter | solution.py:509
  321.4 5.3 %hidden_back.1 = (f32[512,1024]{1,0:T(8,128)S(1)}, bf16[512,1024]{1,0:T(8,128)(2,1)}, f32[2,1024]{1,0:T(2,128)S(1)}) custom-call(bf16[1024,768]{1,0:T(8,128)(2,1)S(1)} %copy-done.14, bf16[1024,768]{1,0:T(8,128)(2,1)S(1)} %copy-done.16, bf16[1024,1536]{1,0:T(8,128)(2,1)S(1)} %copy-done.21, f32[1024,1024]{1,0:T(8,128)S(1)} %copy-done.4), custom_call_target="tpu_custom_call" | custom-call | flops 1048576 | tf_op jit(solution)/shard_map/hidden_back/pallas_call | solution.py:202
  348.8 14.1 %collective-permute-done.25 = bf16[64,1792]{1,0:T(8,128)(2,1)} collective-permute-done((bf16[64,1792]{1,0:T(8,128)(2,1)}, bf16[64,1792]{1,0:T(8,128)(2,1)}, u32[]{:S(2)}, u32[]{:S(2)}) %collective-permute-start.25) | collective-permute-done | bytes 229408 | tf_op jit(solution)/shard_map/ppermute | solution.py:330
  376.3 4.4 %all-to-all-start.3 = ((bf16[16,2,512]{2,1,0:T(2,128)(2,1)}), bf16[16,2,512]{2,1,0:T(2,128)(2,1)}, u32[]{:S(2)}, u32[]{:S(2)}) async-start(bf16[16,2,512]{2,1,0:T(2,128)(2,1)} %reshape.137), calls=%async_computation.4 | async-start | bytes 65536 | tf_op jit(solution)/shard_map/all_to_all | solution.py:572
  394.2 4.5 %multiply_add_fusion = f32[512,1024]{1,0:T(8,128)} fusion(f32[512,1024]{1,0:T(8,128)} %copy-done.35, f32[1024,1024]{1,0:T(8,128)S(1)} %copy-done.5, f32[512]{0:T(512)S(1)} %broadcast_multiply_fusion.1, f32[512]{0:T(512)S(1)} %broadcast_multiply_fusion.2, f32[512]{0:T(512)S(1)} %slice-done, f32[1024]{0:T(1024)S(1)} %bitcast.105, f32[512,1024]{1,0:T(8,128)} %copy-done.12, ...), kind=kLoop, calls=%fused_computation.20 | loop fusion | flops 4194304 | bytes 9447424 | tf_op jit(solution)/shard_map/add | solution.py:577
  (340 shorter events, 167.9 us)
Async XLA Ops:
  7.2 53.6 %all-gather.3.cloned.1.call-start = ((), (), s32[]{:S(2)}) async-start(), calls=%async_computation.5 | async-start | bytes 3342336 | tf_op jit(solution)/shard_map/all_gather | solution.py:410
  9.0 136.2 %all-gather.5.cloned.1.call-start = ((), (), s32[]{:S(2)}) async-start(), calls=%async_computation.6 | async-start | bytes 8912896 | tf_op jit(solution)/shard_map/all_gather | solution.py:412
  9.1 26.4 %collective-permute-start = (bf16[512,1024]{1,0:T(8,128)(2,1)}, bf16[512,1024]{1,0:T(8,128)(2,1)S(1)}, u32[]{:S(2)}, u32[]{:S(2)}) collective-permute-start(bf16[512,1024]{1,0:T(8,128)(2,1)} %bitcast.81), channel_id=1, source_target_pairs={{1,0},{0,1},{3,2},{2,3},{5,4},{4,5},{7,6},{6,7},{9,8},{8,9},{11,10... | collective-permute-start | bytes 3145736 | tf_op jit(solution)/shard_map/ppermute | solution.py:290
  37.7 45.6 %collective-permute-start.4 = (bf16[512,1024]{1,0:T(8,128)(2,1)}, bf16[512,1024]{1,0:T(8,128)(2,1)}, u32[]{:S(2)}, u32[]{:S(2)}) collective-permute-start(bf16[512,1024]{1,0:T(8,128)(2,1)} %bitcast.6), channel_id=1, source_target_pairs={{1,0},{0,1},{3,2},{2,3},{5,4},{4,5},{7,6},{6,7},{9,8},{8,9},{11,10... | collective-permute-start | bytes 3145736 | tf_op jit(solution)/shard_map/ppermute | solution.py:290
  47.0 265.7 %reduce-scatter.2.cloned.1.call-start = ((), (), s32[]{:S(2)}) async-start(), calls=%async_computation.7 | async-start | bytes 4456448 | tf_op jit(solution)/shard_map/reduce_scatter | solution.py:509
  54.2 15.1 %collective-permute-start.2 = (bf16[64,1024]{1,0:T(8,128)(2,1)S(1)}, bf16[64,1024]{1,0:T(8,128)(2,1)S(1)}, u32[]{:S(2)}, u32[]{:S(2)}) collective-permute-start(bf16[64,1024]{1,0:T(8,128)(2,1)S(1)} %copy-done.71), channel_id=1, source_target_pairs={{0,16},{2,18},{4,20},{6,22},{8,24},{10,26},{12,28},{14,30},{16,0},... | collective-permute-start | bytes 393224 | tf_op jit(solution)/shard_map/ppermute | solution.py:330
  55.6 13.7 %collective-permute-start.1 = (bf16[64,1024]{1,0:T(8,128)(2,1)S(1)}, bf16[64,1024]{1,0:T(8,128)(2,1)S(1)}, u32[]{:S(2)}, u32[]{:S(2)}) collective-permute-start(bf16[64,1024]{1,0:T(8,128)(2,1)S(1)} %copy-done.71), channel_id=1, source_target_pairs={{0,8},{2,10},{4,12},{6,14},{8,16},{10,18},{12,20},{14,22},{16,24},... | collective-permute-start | bytes 393224 | tf_op jit(solution)/shard_map/ppermute | solution.py:330
  72.8 24.0 %collective-permute-start.5 = (bf16[4,64,1024]{2,1,0:T(8,128)(2,1)}, bf16[4,64,1024]{2,1,0:T(8,128)(2,1)}, u32[]{:S(2)}, u32[]{:S(2)}) collective-permute-start(bf16[4,64,1024]{2,1,0:T(8,128)(2,1)} %bitcast_dynamic-update-slice_fusion), channel_id=1, source_target_pairs={{0,4},{2,6},{4,0},{6,2},{8,12},{10,14},{12,8},{14,10},{16,20},{18,... | collective-permute-start | bytes 1572872 | tf_op jit(solution)/shard_map/ppermute | solution.py:327
  105.4 14.6 %collective-permute-start.8 = (bf16[512,512]{1,0:T(8,128)(2,1)S(1)}, bf16[512,512]{1,0:T(8,128)(2,1)S(1)}, u32[]{:S(2)}, u32[]{:S(2)}) collective-permute-start(bf16[512,512]{1,0:T(8,128)(2,1)S(1)} %copy-done.30), channel_id=1, source_target_pairs={{1,0},{0,1},{3,2},{2,3},{5,4},{4,5},{7,6},{6,7},{9,8},{8,9},{11,10... | collective-permute-start | bytes 1572872 | tf_op jit(solution)/shard_map/ppermute | solution.py:290
  166.2 25.6 %collective-permute-start.9 = (bf16[512,1024]{1,0:T(8,128)(2,1)}, bf16[512,1024]{1,0:T(8,128)(2,1)}, u32[]{:S(2)}, u32[]{:S(2)}) collective-permute-start(bf16[512,1024]{1,0:T(8,128)(2,1)} %get-tuple-element.164), channel_id=1, source_target_pairs={{0,1},{1,0},{2,3},{3,2},{4,5},{5,4},{6,7},{7,6},{8,9},{9,8},{10,11... | collective-permute-start | bytes 3145736 | tf_op jit(solution)/shard_map/ppermute | solution.py:293
  226.7 31.6 %collective-permute-start.13 = (bf16[256,2048]{1,0:T(8,128)(2,1)S(1)}, bf16[256,2048]{1,0:T(8,128)(2,1)S(1)}, u32[]{:S(2)}, u32[]{:S(2)}) collective-permute-start(bf16[256,2048]{1,0:T(8,128)(2,1)S(1)} %add_convert_fusion.2), channel_id=1, source_target_pairs={{0,4},{2,6},{4,0},{6,2},{8,12},{10,14},{12,8},{14,10},{16,20},{18,... | collective-permute-start | bytes 3145736 | tf_op jit(solution)/shard_map/ppermute | solution.py:327
  227.3 37.1 %collective-permute-start.20 = (bf16[512,1024]{1,0:T(8,128)(2,1)S(1)}, bf16[512,1024]{1,0:T(8,128)(2,1)S(1)}, u32[]{:S(2)}, u32[]{:S(2)}) collective-permute-start(bf16[512,1024]{1,0:T(8,128)(2,1)S(1)} %copy-done.32), channel_id=1, source_target_pairs={{0,1},{1,0},{2,3},{3,2},{4,5},{5,4},{6,7},{7,6},{8,9},{9,8},{10,11... | collective-permute-start | bytes 3145736 | tf_op jit(solution)/shard_map/ppermute | solution.py:293
  228.8 52.0 %collective-permute-start.16 = (bf16[256,1024]{1,0:T(8,128)(2,1)S(1)}, bf16[256,1024]{1,0:T(8,128)(2,1)S(1)}, u32[]{:S(2)}, u32[]{:S(2)}) collective-permute-start(bf16[256,1024]{1,0:T(8,128)(2,1)S(1)} %add_convert_fusion.5), channel_id=1, source_target_pairs={{0,4},{2,6},{4,0},{6,2},{8,12},{10,14},{12,8},{14,10},{16,20},{18,... | collective-permute-start | bytes 1572872 | tf_op jit(solution)/shard_map/ppermute | solution.py:327
  261.7 35.4 %collective-permute-start.15 = (bf16[256,768]{1,0:T(8,128)(2,1)S(1)}, bf16[256,768]{1,0:T(8,128)(2,1)}, u32[]{:S(2)}, u32[]{:S(2)}) collective-permute-start(bf16[256,768]{1,0:T(8,128)(2,1)S(1)} %add_convert_fusion.7), channel_id=1, source_target_pairs={{0,4},{2,6},{4,0},{6,2},{8,12},{10,14},{12,8},{14,10},{16,20},{18,... | collective-permute-start | bytes 1179656 | tf_op jit(solution)/shard_map/ppermute | solution.py:327
  262.7 19.0 %collective-permute-start.19 = (bf16[64,2048]{1,0:T(8,128)(2,1)S(1)}, bf16[64,2048]{1,0:T(8,128)(2,1)S(1)}, u32[]{:S(2)}, u32[]{:S(2)}) collective-permute-start(bf16[64,2048]{1,0:T(8,128)(2,1)S(1)} %get-tuple-element.275), channel_id=1, source_target_pairs={{0,24},{2,26},{4,28},{6,30},{8,0},{10,2},{12,4},{14,6},{16,8},{18,... | collective-permute-start | bytes 786440 | tf_op jit(solution)/shard_map/ppermute | solution.py:330
  262.7 32.9 %collective-permute-start.18 = (bf16[64,2048]{1,0:T(8,128)(2,1)S(1)}, bf16[64,2048]{1,0:T(8,128)(2,1)S(1)}, u32[]{:S(2)}, u32[]{:S(2)}) collective-permute-start(bf16[64,2048]{1,0:T(8,128)(2,1)S(1)} %get-tuple-element.276), channel_id=1, source_target_pairs={{0,16},{2,18},{4,20},{6,22},{8,24},{10,26},{12,28},{14,30},{16,0},... | collective-permute-start | bytes 786440 | tf_op jit(solution)/shard_map/ppermute | solution.py:330
  264.4 32.0 %collective-permute-start.17 = (bf16[64,2048]{1,0:T(8,128)(2,1)S(1)}, bf16[64,2048]{1,0:T(8,128)(2,1)S(1)}, u32[]{:S(2)}, u32[]{:S(2)}) collective-permute-start(bf16[64,2048]{1,0:T(8,128)(2,1)S(1)} %get-tuple-element.277), channel_id=1, source_target_pairs={{0,8},{2,10},{4,12},{6,14},{8,16},{10,18},{12,20},{14,22},{16,24},... | collective-permute-start | bytes 786440 | tf_op jit(solution)/shard_map/ppermute | solution.py:330
  328.3 16.0 %collective-permute-start.23 = (bf16[256,768]{1,0:T(8,128)(2,1)}, bf16[256,768]{1,0:T(8,128)(2,1)}, u32[]{:S(2)}, u32[]{:S(2)}) collective-permute-start(bf16[256,768]{1,0:T(8,128)(2,1)} %add_convert_fusion.6), channel_id=1, source_target_pairs={{0,4},{2,6},{4,0},{6,2},{8,12},{10,14},{12,8},{14,10},{16,20},{18,... | collective-permute-start | bytes 1179656 | tf_op jit(solution)/shard_map/ppermute | solution.py:327
  342.4 20.4 %collective-permute-start.25 = (bf16[64,1792]{1,0:T(8,128)(2,1)}, bf16[64,1792]{1,0:T(8,128)(2,1)}, u32[]{:S(2)}, u32[]{:S(2)}) collective-permute-start(bf16[64,1792]{1,0:T(8,128)(2,1)} %get-tuple-element.287), channel_id=1, source_target_pairs={{0,16},{2,18},{4,20},{6,22},{8,24},{10,26},{12,28},{14,30},{16,0},... | collective-permute-start | bytes 688136 | tf_op jit(solution)/shard_map/ppermute | solution.py:330
  342.4 20.4 %collective-permute-start.24 = (bf16[64,1792]{1,0:T(8,128)(2,1)}, bf16[64,1792]{1,0:T(8,128)(2,1)}, u32[]{:S(2)}, u32[]{:S(2)}) collective-permute-start(bf16[64,1792]{1,0:T(8,128)(2,1)} %get-tuple-element.288), channel_id=1, source_target_pairs={{0,8},{2,10},{4,12},{6,14},{8,16},{10,18},{12,20},{14,22},{16,24},... | collective-permute-start | bytes 688136 | tf_op jit(solution)/shard_map/ppermute | solution.py:330
  343.5 47.0 %collective-permute-start.30 = (bf16[512,1024]{1,0:T(8,128)(2,1)}, bf16[512,1024]{1,0:T(8,128)(2,1)}, u32[]{:S(2)}, u32[]{:S(2)}) collective-permute-start(bf16[512,1024]{1,0:T(8,128)(2,1)} %get-tuple-element.236), channel_id=1, source_target_pairs={{0,1},{1,0},{2,3},{3,2},{4,5},{5,4},{6,7},{7,6},{8,9},{9,8},{10,11... | collective-permute-start | bytes 3145736 | tf_op jit(solution)/shard_map/ppermute | solution.py:293
  366.7 32.0 %collective-permute-start.29 = (bf16[64,768]{1,0:T(8,128)(2,1)}, bf16[64,768]{1,0:T(8,128)(2,1)}, u32[]{:S(2)}, u32[]{:S(2)}) collective-permute-start(bf16[64,768]{1,0:T(8,128)(2,1)} %get-tuple-element.291), channel_id=1, source_target_pairs={{0,24},{2,26},{4,28},{6,30},{8,0},{10,2},{12,4},{14,6},{16,8},{18,... | collective-permute-start | bytes 294920 | tf_op jit(solution)/shard_map/ppermute | solution.py:330
  366.7 32.0 %collective-permute-start.28 = (bf16[64,768]{1,0:T(8,128)(2,1)}, bf16[64,768]{1,0:T(8,128)(2,1)}, u32[]{:S(2)}, u32[]{:S(2)}) collective-permute-start(bf16[64,768]{1,0:T(8,128)(2,1)} %get-tuple-element.292), channel_id=1, source_target_pairs={{0,16},{2,18},{4,20},{6,22},{8,24},{10,26},{12,28},{14,30},{16,0},... | collective-permute-start | bytes 294920 | tf_op jit(solution)/shard_map/ppermute | solution.py:330
  369.3 29.4 %collective-permute-start.27 = (bf16[64,768]{1,0:T(8,128)(2,1)}, bf16[64,768]{1,0:T(8,128)(2,1)}, u32[]{:S(2)}, u32[]{:S(2)}) collective-permute-start(bf16[64,768]{1,0:T(8,128)(2,1)} %get-tuple-element.293), channel_id=1, source_target_pairs={{0,8},{2,10},{4,12},{6,14},{8,16},{10,18},{12,20},{14,22},{16,24},... | collective-permute-start | bytes 294920 | tf_op jit(solution)/shard_map/ppermute | solution.py:330
  (93 other events, 992.8 us)
Sparse Core Ops, SparseCore 0:
  10.9 48.9 all-gather.2
  62.6 82.5 all-gather.4
  215.0 97.6 reduce-scatter.1

commit v2 on v1

--- a/solution.py
+++ b/solution.py
@@ -182,6 +182,42 @@
     )(place, value)
 
 
+def divisor(count):
+    return next(size for size in (512, 384, 256, 128) if count % size == 0)
+
+
+def mat_kernel(left_ref, right_ref, out_ref):
+    out_ref[...] = mm(left_ref[...], right_ref[...]).astype(out_ref.dtype)
+
+
+def mat_turned_kernel(left_ref, right_ref, out_ref, turned):
+    @pl.when(pl.program_id(0) == 0)
+    def _():
+        turned[...] = left_ref[...].T
+
+    out_ref[...] = mm(turned[...], right_ref[...]).astype(out_ref.dtype)
+
+
+def mat(left, right, part=0, parts=1, turned=False):
+    depth, columns = right.shape
+    rows = left.shape[1] if turned else left.shape[0] // parts
+    block = divisor(columns)
+    return pl.pallas_call(
+        mat_turned_kernel if turned else mat_kernel,
+        grid=(columns // block,),
+        in_specs=[
+            pl.BlockSpec((depth, rows) if turned else (rows, depth), lambda j: (part, 0)),
+            pl.BlockSpec((depth, block), lambda j: (0, j)),
+        ],
+        out_specs=pl.BlockSpec((rows, block), lambda j: (0, j)),
+        out_shape=jax.ShapeDtypeStruct((rows, columns), jnp.bfloat16),
+        scratch_shapes=[pltpu.VMEM((rows, depth), jnp.bfloat16)] if turned else [],
+        compiler_params=pltpu.CompilerParams(vmem_limit_bytes=18 * MIB),
+        cost_estimate=pl.CostEstimate(flops=rows * depth, bytes_accessed=0, transcendentals=0),
+        name="mat",
+    )(left, right)
+
+
 def hidden_back_kernel(groups, *refs):
     values, (weight_ref, normed_ref, own_ref, peers_ref, sums_ref) = refs[:groups], refs[groups:]
     size = values[0].shape[1]
@@ -360,9 +396,7 @@
     place = place.astype(jnp.int32)
 
     def scatter_core(turned, value):
-        half = turned.shape[0] // 2
-        other = mm(turned[half:], value).astype(low)
-        return mm(turned[:half], value).astype(low), core_swap(other)
+        return mat(turned, value, 0, 2), core_swap(mat(turned, value, 1, 2))
 
     def x_part(pair):
         half = pair[0].shape[0] // 2
@@ -484,7 +518,11 @@
             own = own + value.astype(wide)
         return own
 
-    grad_sent, act, grad_up, branch_parts = after((grad_sent, act, grad_up, branch_parts))
+    term_down = mat(grad_rows, act, turned=True)
+    grad_sent, term_down, act, grad_up, branch_parts = after(
+        (grad_sent, term_down, act, grad_up, branch_parts)
+    )
+    grad_w_down = lax.psum_scatter(term_down, "fsdp", scatter_dimension=0, tiled=True)
     grad_hidden_two = add_parts(grad_parts[0], grad_sent)
     grad_mixed = own_cotangent.astype(wide)
     grad_shift_two = jnp.sum(grad_hidden_two, 0)
@@ -502,16 +540,11 @@
         for r in range(splits)
     ]
     grad_arrived = [send(grad_pieces[r], r) for r in range(1, splits)]
-    term_down = mm(grad_rows, act, TN).astype(low)
-    grad_arrived, branch_parts, term_down, act, grad_up = after(
-        (grad_arrived, branch_parts, term_down, act, grad_up)
-    )
-    grad_w_down = lax.psum_scatter(term_down, "fsdp", scatter_dimension=0, tiled=True)
     up_pair = scatter_core(turned_two, grad_up)
     out_pair = scatter_core(turned_attn, grad_branch_one)
     up_part, out_part = x_part(up_pair), x_part(out_pair)
-    up_pair, out_pair, up_part, out_part, grad_arrived = after(
-        (up_pair, out_pair, up_part, out_part, grad_arrived)
+    up_pair, out_pair, up_part, out_part, grad_arrived, branch_parts = after(
+        (up_pair, out_pair, up_part, out_part, grad_arrived, branch_parts)
     )
     up_terms = scatter_x(up_pair, up_part)
     branch_sent = send_parts(branch_parts)
@@ -527,26 +560,22 @@
         value = attend_back(qkv, grad_heads, lse, group * each, each)
         values.append(value)
         if group + 1 < groups:
-            values, up_terms = after((values, up_terms))
             pair = scatter_core(turned_one, values[0])
-            up_pieces = scatter_z(up_terms)
             part = x_part(pair)
-            pair, part, grad_heads, lse = after((pair, part, grad_heads, lse))
+            pair, part, grad_heads, lse, up_terms = after(
+                (pair, part, grad_heads, lse, up_terms)
+            )
             first_terms = scatter_x(pair, part)
-    if groups == 1:
-        up_pieces = scatter_z(up_terms)
-    values, first_terms, out_terms, up_pieces, branch_sent, grad_w_down = after(
-        (values, first_terms, out_terms, up_pieces, branch_sent, grad_w_down)
+    up_pieces = scatter_z(up_terms)
+    values, first_terms, out_terms, branch_sent = after(
+        (values, first_terms, out_terms, branch_sent)
     )
     pair = scatter_core(turned_one, values[-1])
     part = x_part(pair)
     pair, part, values = after((pair, part, values))
     last_terms = scatter_x(pair, part)
     own_grad, peers_grad, sums = hidden_back(values, qkv_half, normed_all, tokens)
-    own_grad, peers_grad, sums, first_terms, out_terms = after(
-        (own_grad, peers_grad, sums, first_terms, out_terms)
-    )
-    joint_pieces = scatter_z(*([out_terms, first_terms] if groups > 1 else [out_terms]))
+    own_grad, peers_grad, sums, last_terms = after((own_grad, peers_grad, sums, last_terms))
     branch_two = add_parts(branch_parts[0], branch_sent)
     grad_gate_two = jnp.sum(grad_mixed * branch_two, 0)
 
@@ -560,16 +589,18 @@
     grad_mod, hidden_parts = after((grad_mod, hidden_parts))
     grad_mod_cols = lax.all_to_all(grad_mod, "fsdp", split_axis=1, concat_axis=0, tiled=True)
     hidden_sent = send_parts(hidden_parts)
-    grad_mod_cols, last_terms, up_pieces, grad_w_down = after(
-        (grad_mod_cols, last_terms, up_pieces, grad_w_down)
-    )
     last_pieces = scatter_z(last_terms)
+    grad_mod_cols, first_terms, out_terms = after((grad_mod_cols, first_terms, out_terms))
+    joint_pieces = scatter_z(*([out_terms, first_terms] if groups > 1 else [out_terms]))
     grad_w_ada = mm(cond_all, grad_mod_cols, TN)
     grad_b_ada = jnp.sum(grad_mod_cols.astype(wide), 0)
     cond_term = mm(grad_mod_cols, w_ada, NT).astype(low)
-    cond_term, middle, joint_pieces = after((cond_term, middle, joint_pieces))
+    cond_term, middle, grad_w_down, last_pieces, hidden_sent, up_pieces = after(
+        (cond_term, middle, grad_w_down, last_pieces, hidden_sent, up_pieces)
+    )
     mixed = (middle + gate_two * branch_two).astype(low)
     cond_terms = lax.all_to_all(cond_term, "fsdp", split_axis=0, concat_axis=0, tiled=True)
+    cond_terms, joint_pieces = after((cond_terms, joint_pieces))
     grad_w_up = scatter_end(up_pieces)
     grad_joint = scatter_end(joint_pieces).astype(low)
     grad_w_out = seq_sum(grad_joint[:, :width])

time: 419 us -> 408 us (0.974)
  waiting for transfers between devices: 116 us -> 90.7 us
  Pallas kernels: 87.1 us -> 109 us
  matrix products: 34.3 us -> 13.6 us
  starting transfers between devices: 50.6 us -> 59 us
    ppermute x12, waiting for transfers between devices: 33.7 us -> 8.98 us  [z_send(): lax.ppermute(value, 'fsdp', [(i, (i + 4 * step) % shards) for i in range(...]
    pallas_call x0 -> x9, Pallas kernels: none -> 24.1 us  [mat(): pl.pallas_call(mat_turned_kernel if turned else mat_kernel, grid=(columns...]
    dot_general x16 -> x7, matrix products: 34.3 us -> 13.6 us  [mm(): return lax.dot_general(a, b, dims, preferred_element_type=jnp.float32)]
    ppermute x12, starting transfers between devices: 14.6 us -> 21.7 us  [z_send(): lax.ppermute(value, 'fsdp', [(i, (i + 4 * step) % shards) for i in range(...]
    ppermute x4, waiting for transfers between devices: 12.3 us -> 6.02 us  [send(): lax.ppermute(value, 'seq', [(i, (i + step) % splits) for i in range(split...]
    ppermute x7, waiting for transfers between devices: 14.2 us -> 19.5 us  [fetch(): lax.ppermute(value, 'seq', [((i + step) % splits, i) for i in range(split...]
    unnamed x170 -> x167, local copies, waits for them, and re-layouts: 31.4 us -> 36.1 us
    all_to_all x1, waiting for transfers between devices: 0.07 us -> 4.77 us  [per_device(): lax.all_to_all(grad_mod, 'fsdp', split_axis=1, concat_axis=0, tiled=True)]
  transfers between devices with their start and end apart: 39 -> 39, of which waited for: 18 -> 15; matrix products, arithmetic and copies ran while one was open for 22% -> 20% of each run, Pallas kernels for 16% -> 22%
where the time goes in v2:
time: 408 us; the launch traced here: 403 us
  Pallas kernels  109 us (27%)
  waiting for transfers between devices  90.7 us (22%)
  starting transfers between devices  59 us (14%)
  other arithmetic  59 us (14%)
  local copies, waits for them, and re-layouts  44.1 us (11%)
  between operations  15.5 us (4%)
  matrix products  13.6 us (3%)
  blocking collectives  12.4 us (3%)
    unnamed x167, local copies, waits for them, and re-layouts  36.1 us
    pallas_call x2, Pallas kernels, feed(): pl.pallas_call(partial(feed_kernel, int(aliased)), grid=(count,), in_spec...  28.8 us
    pallas_call x2, Pallas kernels, attend_back(): pl.pallas_call(partial(attend_back_kernel, len(grad_pieces)), grid=(pairs...  25.4 us
    pallas_call x9, Pallas kernels, mat(): pl.pallas_call(mat_turned_kernel if turned else mat_kernel, grid=(columns...  24.1 us
    ppermute x12, starting transfers between devices, z_send(): lax.ppermute(value, 'fsdp', [(i, (i + 4 * step) % shards) for i in range(...  21.7 us
    all_gather x1, waiting for transfers between devices, per_device(): lax.all_gather(jnp.concatenate([up_shard, down_shard.T], 1), 'fsdp', axis...  21.3 us
    pallas_call x2, Pallas kernels, attend(): pl.pallas_call(attend_kernel, grid=(pairs, count), in_specs=[pl.BlockSpec...  19.9 us
    ppermute x7, waiting for transfers between devices, fetch(): lax.ppermute(value, 'seq', [((i + step) % splits, i) for i in range(split...  19.5 us
  transfers between devices with their start and end apart: 39, of which 15 were waited for; matrix products, arithmetic and copies ran while one was open for 20% of the time, Pallas kernels for 22%

profile of v2, /device:TPU:0, one launch (start us, length us, event | category | flops | bytes accessed | tf_op | source)
XLA Modules:
  0.0 403.1 jit_solution(16634854192680464102)
XLA Ops:
  14.4 12.4 %all_to_all.50 = bf16[16,2,512]{2,1,0:T(2,128)(2,1)S(1)} all-to-all(bf16[16,2,512]{2,1,0:T(2,128)(2,1)S(1)} %reshape.130), channel_id=1, replica_groups=mesh['fsdp'=16,'seq'=2] {'fsdp'}, dimensions={0} | all-to-all | bytes 65536 | tf_op jit(solution)/shard_map/all_to_all | solution.py:424
  26.8 8.7 %collective-permute-done = bf16[512,1024]{1,0:T(8,128)(2,1)S(1)} collective-permute-done((bf16[512,1024]{1,0:T(8,128)(2,1)}, bf16[512,1024]{1,0:T(8,128)(2,1)S(1)}, u32[]{:S(2)}, u32[]{:S(2)}) %collective-permute-start) | collective-permute-done | bytes 1048608 | tf_op jit(solution)/shard_map/ppermute | solution.py:326
  41.2 5.9 %all-to-all-start.1 = ((bf16[16,2,192]{2,1,0:T(2,128)(2,1)}), bf16[16,2,192]{2,1,0:T(2,128)(2,1)S(1)}, u32[]{:S(2)}, u32[]{:S(2)}) async-start(bf16[16,2,192]{2,1,0:T(2,128)(2,1)} %reshape.132), calls=%async_computation.1 | async-start | bytes 32768 | tf_op jit(solution)/shard_map/all_to_all | solution.py:434
  48.2 5.3 %all-to-all-done.1 = bf16[16,2,192]{2,1,0:T(2,128)(2,1)S(1)} async-done(((bf16[16,2,192]{2,1,0:T(2,128)(2,1)}), bf16[16,2,192]{2,1,0:T(2,128)(2,1)S(1)}, u32[]{:S(2)}, u32[]{:S(2)}) %all-to-all-start.1) | async-done | bytes 12320 | tf_op jit(solution)/shard_map/all_to_all | solution.py:434
  56.3 4.6 %fusion = (f32[1024,1024]{1,0:T(8,128)}, bf16[1024,1024]{1,0:T(8,128)(2,1)S(1)}) fusion(f32[1024]{0:T(1024)S(1)} %add_rsqrt_fusion, f32[1024]{0:T(1024)S(1)} %broadcast_multiply_fusion, bf16[512,1024]{1,0:T(8,128)(2,1)} %copy-done.52, bf16[512,1024]{1,0:T(8,128)(2,1)} %bitcast.75, f32[1024]{0:T(1024)S(1)} %bitcast.109, f32[1024]{0:T(1024)S(1)} %bitcast.97), kind=kLoop, calls=%fused_computation.2 | loop fusion | flops 9437184 | bytes 8404992 | tf_op jit(solution)/shard_map/mul | solution.py:32
  60.9 6.2 %convolution_convert_fusion.query_ref.all_ref = bf16[1024,1536]{1,0:T(8,128)(2,1)S(1)} fusion(bf16[1024,1024]{1,0:T(8,128)(2,1)S(1)} %get-tuple-element.266.value_ref, bf16[1024,1536]{1,0:T(8,128)(2,1)} %all-gather.3.cloned.1.call-done.refs_2_), kind=kOutput, calls=%fused_computation.7 | convolution fusion | flops 3222798336 | bytes 8388608 | tf_op jit(solution)/shard_map/dot_general | solution.py:26
  70.1 9.9 %attend.2 = (bf16[512,512]{1,0:T(8,128)(2,1)S(1)}, f32[4,2,512]{2,1,0:T(2,128)S(1)}) custom-call(bf16[1024,1536]{1,0:T(8,128)(2,1)S(1)} %convolution_convert_fusion.query_ref.all_ref, bf16[1024,1536]{1,0:T(8,128)(2,1)S(1)} %convolution_convert_fusion.query_ref.all_ref), custom_call_target="tpu_custom_call" | custom-call | flops 2097152 | tf_op jit(solution)/shard_map/attend/pallas_call | solution.py:68
  83.6 9.9 %attend.3 = (bf16[512,512]{1,0:T(8,128)(2,1)S(1)}, f32[4,2,512]{2,1,0:T(2,128)S(1)}) custom-call(bf16[1024,1536]{1,0:T(8,128)(2,1)S(1)} %copy-done.2, bf16[1024,1536]{1,0:T(8,128)(2,1)S(1)} %copy-done.2), custom_call_target="tpu_custom_call" | custom-call | flops 2097152 | tf_op jit(solution)/shard_map/attend/pallas_call | solution.py:68
  124.0 21.3 %all-gather.5.cloned.1.call-done.up_ref.down_ref = bf16[1024,4096]{1,0:T(8,128)(2,1)} async-done(((bf16[64,4096]{1,0:T(8,128)(2,1)}), bf16[1024,4096]{1,0:T(8,128)(2,1)}) %all-gather.5.cloned.1.call-update) | async-done | bytes 8388624 | tf_op jit(solution)/shard_map/all_gather | solution.py:446
  148.1 14.6 %feed.2 = (bf16[1024,2048]{1,0:T(8,128)(2,1)S(1)}, bf16[1024,2048]{1,0:T(8,128)(2,1)S(1)}, bf16[512,1024]{1,0:T(8,128)(2,1)S(1)}, bf16[512,1024]{1,0:T(8,128)(2,1)}) custom-call(bf16[512,1024]{1,0:T(8,128)(2,1)S(1)} %copy-done.27, bf16[1024,1024]{1,0:T(8,128)(2,1)S(1)} %copy-done.8, bf16[1024,4096]{1,0:T(8,128)(2,1)} %all-gather.5.cloned.1.call-done.up_ref.down_ref, ...), custom_call_target="tpu_custom_call" | custom-call | flops 1048576 | tf_op jit(solution)/shard_map/feed/pallas_call | solution.py:135
  166.2 14.1 %feed.3 = (bf16[1024,2048]{1,0:T(8,128)(2,1)S(1)}, bf16[1024,2048]{1,0:T(8,128)(2,1)}, f32[512,1024]{1,0:T(8,128)S(1)}, f32[512,1024]{1,0:T(8,128)S(1)}) custom-call(bf16[512,1024]{1,0:T(8,128)(2,1)S(1)} %copy-done.19, bf16[1024,1024]{1,0:T(8,128)(2,1)S(1)} %copy-done.9, ...), custom_call_target="tpu_custom_call", output_to_operand_aliasing={{0}: (4, {}), {1}: (5, {})} | custom-call | flops 1048576 | tf_op jit(solution)/shard_map/feed/pallas_call | solution.py:135
  183.0 6.3 %mat.9 = bf16[1024,2048]{1,0:T(8,128)(2,1)S(1)} custom-call(bf16[1024,1024]{1,0:T(8,128)(2,1)S(1)} %copy-done.9, bf16[1024,2048]{1,0:T(8,128)(2,1)S(1)} %get-tuple-element.162.right_ref), custom_call_target="tpu_custom_call" | custom-call | flops 1048576 | tf_op jit(solution)/shard_map/mat/pallas_call | solution.py:205
  223.2 5.1 %collective-permute-done.12.rest_1_ = bf16[512,512]{1,0:T(8,128)(2,1)S(1)} collective-permute-done((bf16[512,512]{1,0:T(8,128)(2,1)S(1)}, bf16[512,512]{1,0:T(8,128)(2,1)S(1)}, u32[]{:S(2)}, u32[]{:S(2)}) %collective-permute-start.12) | collective-permute-done | bytes 524320 | tf_op jit(solution)/shard_map/ppermute | solution.py:329
  228.8 12.6 %attend_back.2.right_ref.refs_0_ = bf16[1024,768]{1,0:T(8,128)(2,1)S(1)} custom-call(bf16[1024,1536]{1,0:T(8,128)(2,1)S(1)} %copy-done.3, f32[4,2,1024]{2,1,0:T(2,128)S(1)} %constant_dynamic-update-slice_fusion.lse_ref, bf16[512,512]{1,0:T(8,128)(2,1)S(1)} %get-tuple-element.177.rest_0_, bf16[512,512]{1,0:T(8,128)(2,1)S(1)} %collective-permute-done.12.rest_1_), custom_call_target="tpu_custom_call" | custom-call | flops 2097152 | tf_op jit(solution)/shard_map/attend_back/pallas_call | solution.py:293
  247.1 7.2 %collective-permute-done.14 = bf16[256,2048]{1,0:T(8,128)(2,1)S(1)} collective-permute-done((bf16[256,2048]{1,0:T(8,128)(2,1)S(1)}, bf16[256,2048]{1,0:T(8,128)(2,1)S(1)}, u32[]{:S(2)}, u32[]{:S(2)}) %collective-permute-start.14) | collective-permute-done | bytes 1048608 | tf_op jit(solution)/shard_map/ppermute | solution.py:363
  255.0 12.8 %attend_back.3.right_ref.refs_1_ = bf16[1024,768]{1,0:T(8,128)(2,1)S(1)} custom-call(bf16[1024,1536]{1,0:T(8,128)(2,1)S(1)} %copy-done.3, f32[4,2,1024]{2,1,0:T(2,128)S(1)} %constant_dynamic-update-slice_fusion.lse_ref, bf16[512,512]{1,0:T(8,128)(2,1)S(1)} %get-tuple-element.177.rest_0_, bf16[512,512]{1,0:T(8,128)(2,1)S(1)} %collective-permute-done.12.rest_1_), custom_call_target="tpu_custom_call" | custom-call | flops 2097152 | tf_op jit(solution)/shard_map/attend_back/pallas_call | solution.py:293
  288.2 4.7 %hidden_back.1 = (f32[512,1024]{1,0:T(8,128)S(1)}, bf16[512,1024]{1,0:T(8,128)(2,1)S(1)}, f32[2,1024]{1,0:T(2,128)S(1)}) custom-call(bf16[1024,768]{1,0:T(8,128)(2,1)S(1)} %copy-done.11, bf16[1024,768]{1,0:T(8,128)(2,1)S(1)} %copy-done.13, bf16[1024,1536]{1,0:T(8,128)(2,1)S(1)} %copy-done.39, f32[1024,1024]{1,0:T(8,128)S(1)} %copy-done.7), custom_call_target="tpu_custom_call" | custom-call | flops 1048576 | tf_op jit(solution)/shard_map/hidden_back/pallas_call | solution.py:238
  299.8 4.8 %all-to-all-start.2 = ((bf16[16,2,192]{2,1,0:T(2,128)(2,1)}), bf16[16,2,192]{2,1,0:T(2,128)(2,1)S(1)}, u32[]{:S(2)}, u32[]{:S(2)}) async-start(bf16[16,2,192]{2,1,0:T(2,128)(2,1)} %reshape.134), calls=%async_computation.2 | async-start | bytes 32768 | tf_op jit(solution)/shard_map/all_to_all | solution.py:590
  312.3 4.8 %all-to-all-done.2 = bf16[16,2,192]{2,1,0:T(2,128)(2,1)S(1)} async-done(((bf16[16,2,192]{2,1,0:T(2,128)(2,1)}), bf16[16,2,192]{2,1,0:T(2,128)(2,1)S(1)}, u32[]{:S(2)}, u32[]{:S(2)}) %all-to-all-start.2) | async-done | bytes 12320 | tf_op jit(solution)/shard_map/all_to_all | solution.py:590
  323.8 7.6 %collective-permute-start.22 = (bf16[64,768]{1,0:T(8,128)(2,1)S(1)}, bf16[64,768]{1,0:T(8,128)(2,1)}, u32[]{:S(2)}, u32[]{:S(2)}) collective-permute-start(bf16[64,768]{1,0:T(8,128)(2,1)S(1)} %copy-done.71), channel_id=1, source_target_pairs={{0,16},{2,18},{4,20},{6,22},{8,24},{10,26},{12,28},{14,30},{16,0},... | collective-permute-start | bytes 294920 | tf_op jit(solution)/shard_map/ppermute | solution.py:366
  335.9 6.8 %collective-permute-done.22 = bf16[64,768]{1,0:T(8,128)(2,1)} collective-permute-done((bf16[64,768]{1,0:T(8,128)(2,1)S(1)}, bf16[64,768]{1,0:T(8,128)(2,1)}, u32[]{:S(2)}, u32[]{:S(2)}) %collective-permute-start.22) | collective-permute-done | bytes 98336 | tf_op jit(solution)/shard_map/ppermute | solution.py:366
  343.0 14.1 %reduce-scatter.2.cloned.1.call-done = bf16[64,2048]{1,0:T(8,128)(2,1)} async-done(((bf16[1024,2048]{1,0:T(8,128)(2,1)}), bf16[64,2048]{1,0:T(8,128)(2,1)}) %reduce-scatter.2.cloned.1.call-update) | async-done | bytes 262160 | tf_op jit(solution)/shard_map/reduce_scatter | solution.py:525
  361.6 7.1 %all-to-all-start.3 = ((bf16[16,2,512]{2,1,0:T(2,128)(2,1)}), bf16[16,2,512]{2,1,0:T(2,128)(2,1)}, u32[]{:S(2)}, u32[]{:S(2)}) async-start(bf16[16,2,512]{2,1,0:T(2,128)(2,1)} %reshape.136), calls=%async_computation.4 | async-start | bytes 65536 | tf_op jit(solution)/shard_map/all_to_all | solution.py:602
  372.7 4.5 %multiply_add_fusion = f32[512,1024]{1,0:T(8,128)} fusion(f32[512,1024]{1,0:T(8,128)} %copy-done.49, f32[1024,1024]{1,0:T(8,128)} %get-tuple-element.265.refs_3_, f32[512]{0:T(512)S(1)} %broadcast_multiply_fusion.1, f32[512]{0:T(512)S(1)} %broadcast_multiply_fusion.2, f32[512]{0:T(512)S(1)} %slice-done, f32[1024]{0:T(1024)S(1)} %bitcast.99, ...), kind=kLoop, calls=%fused_computation.17 | loop fusion | flops 4194304 | bytes 9447424 | tf_op jit(solution)/shard_map/add | solution.py:608
  (337 shorter events, 176.1 us)
Async XLA Ops:
  7.2 53.7 %all-gather.3.cloned.1.call-start = ((), (), s32[]{:S(2)}) async-start(), calls=%async_computation.5 | async-start | bytes 3342336 | tf_op jit(solution)/shard_map/all_gather | solution.py:444
  9.0 136.3 %all-gather.5.cloned.1.call-start = ((), (), s32[]{:S(2)}) async-start(), calls=%async_computation.6 | async-start | bytes 8912896 | tf_op jit(solution)/shard_map/all_gather | solution.py:446
  9.1 26.4 %collective-permute-start = (bf16[512,1024]{1,0:T(8,128)(2,1)}, bf16[512,1024]{1,0:T(8,128)(2,1)S(1)}, u32[]{:S(2)}, u32[]{:S(2)}) collective-permute-start(bf16[512,1024]{1,0:T(8,128)(2,1)} %bitcast.74), channel_id=1, source_target_pairs={{1,0},{0,1},{3,2},{2,3},{5,4},{4,5},{7,6},{6,7},{9,8},{8,9},{11,10... | collective-permute-start | bytes 3145736 | tf_op jit(solution)/shard_map/ppermute | solution.py:326
  37.7 42.3 %collective-permute-start.4 = (bf16[512,1024]{1,0:T(8,128)(2,1)}, bf16[512,1024]{1,0:T(8,128)(2,1)}, u32[]{:S(2)}, u32[]{:S(2)}) collective-permute-start(bf16[512,1024]{1,0:T(8,128)(2,1)} %bitcast.6), channel_id=1, source_target_pairs={{1,0},{0,1},{3,2},{2,3},{5,4},{4,5},{7,6},{6,7},{9,8},{8,9},{11,10... | collective-permute-start | bytes 3145736 | tf_op jit(solution)/shard_map/ppermute | solution.py:326
  47.1 310.1 %reduce-scatter.2.cloned.1.call-start = ((), (), s32[]{:S(2)}) async-start(), calls=%async_computation.7 | async-start | bytes 4456448 | tf_op jit(solution)/shard_map/reduce_scatter | solution.py:525
  54.3 15.0 %collective-permute-start.2 = (bf16[64,1024]{1,0:T(8,128)(2,1)S(1)}, bf16[64,1024]{1,0:T(8,128)(2,1)S(1)}, u32[]{:S(2)}, u32[]{:S(2)}) collective-permute-start(bf16[64,1024]{1,0:T(8,128)(2,1)S(1)} %copy-done.69), channel_id=1, source_target_pairs={{0,16},{2,18},{4,20},{6,22},{8,24},{10,26},{12,28},{14,30},{16,0},... | collective-permute-start | bytes 393224 | tf_op jit(solution)/shard_map/ppermute | solution.py:366
  69.4 24.1 %collective-permute-start.5 = (bf16[4,64,1024]{2,1,0:T(8,128)(2,1)S(1)}, bf16[4,64,1024]{2,1,0:T(8,128)(2,1)S(1)}, u32[]{:S(2)}, u32[]{:S(2)}) collective-permute-start(bf16[4,64,1024]{2,1,0:T(8,128)(2,1)S(1)} %bitcast_dynamic-update-slice_fusion), channel_id=1, source_target_pairs={{0,4},{2,6},{4,0},{6,2},{8,12},{10,14},{12,8},{14,10},{16,20},{18,... | collective-permute-start | bytes 1572872 | tf_op jit(solution)/shard_map/ppermute | solution.py:363
  164.7 26.6 %collective-permute-start.9 = (bf16[512,1024]{1,0:T(8,128)(2,1)}, bf16[512,1024]{1,0:T(8,128)(2,1)}, u32[]{:S(2)}, u32[]{:S(2)}) collective-permute-start(bf16[512,1024]{1,0:T(8,128)(2,1)} %get-tuple-element.161), channel_id=1, source_target_pairs={{0,1},{1,0},{2,3},{3,2},{4,5},{5,4},{6,7},{7,6},{8,9},{9,8},{10,11... | collective-permute-start | bytes 3145736 | tf_op jit(solution)/shard_map/ppermute | solution.py:329
  199.1 22.4 %collective-permute-start.10 = (bf16[512,2048]{1,0:T(8,128)(2,1)}, bf16[512,2048]{1,0:T(8,128)(2,1)}, u32[]{:S(2)}, u32[]{:S(2)}) collective-permute-start(bf16[512,2048]{1,0:T(8,128)(2,1)} %mat.11), channel_id=1, source_target_pairs={{0,2},{2,0},{4,6},{6,4},{8,10},{10,8},{12,14},{14,12},{16,18},{18,... | collective-permute-start | bytes 6291464 | tf_op jit(solution)/shard_map/ppermute | solution.py:360
  228.2 26.1 %collective-permute-start.14 = (bf16[256,2048]{1,0:T(8,128)(2,1)S(1)}, bf16[256,2048]{1,0:T(8,128)(2,1)S(1)}, u32[]{:S(2)}, u32[]{:S(2)}) collective-permute-start(bf16[256,2048]{1,0:T(8,128)(2,1)S(1)} %add_convert_fusion.2), channel_id=1, source_target_pairs={{0,4},{2,6},{4,0},{6,2},{8,12},{10,14},{12,8},{14,10},{16,20},{18,... | collective-permute-start | bytes 3145736 | tf_op jit(solution)/shard_map/ppermute | solution.py:363
  243.2 25.6 %collective-permute-start.17 = (bf16[512,1024]{1,0:T(8,128)(2,1)S(1)}, bf16[512,1024]{1,0:T(8,128)(2,1)S(1)}, u32[]{:S(2)}, u32[]{:S(2)}) collective-permute-start(bf16[512,1024]{1,0:T(8,128)(2,1)S(1)} %copy-done.44), channel_id=1, source_target_pairs={{0,1},{1,0},{2,3},{3,2},{4,5},{5,4},{6,7},{7,6},{8,9},{9,8},{10,11... | collective-permute-start | bytes 3145736 | tf_op jit(solution)/shard_map/ppermute | solution.py:329
  243.8 24.0 %collective-permute-start.16 = (bf16[256,1024]{1,0:T(8,128)(2,1)S(1)}, bf16[256,1024]{1,0:T(8,128)(2,1)S(1)}, u32[]{:S(2)}, u32[]{:S(2)}) collective-permute-start(bf16[256,1024]{1,0:T(8,128)(2,1)S(1)} %add_convert_fusion.5), channel_id=1, source_target_pairs={{0,4},{2,6},{4,0},{6,2},{8,12},{10,14},{12,8},{14,10},{16,20},{18,... | collective-permute-start | bytes 1572872 | tf_op jit(solution)/shard_map/ppermute | solution.py:363
  254.3 17.8 %collective-permute-start.15 = (bf16[256,768]{1,0:T(8,128)(2,1)S(1)}, bf16[256,768]{1,0:T(8,128)(2,1)S(1)}, u32[]{:S(2)}, u32[]{:S(2)}) collective-permute-start(bf16[256,768]{1,0:T(8,128)(2,1)S(1)} %add_convert_fusion.7), channel_id=1, source_target_pairs={{0,4},{2,6},{4,0},{6,2},{8,12},{10,14},{12,8},{14,10},{16,20},{18,... | collective-permute-start | bytes 1179656 | tf_op jit(solution)/shard_map/ppermute | solution.py:363
  281.8 42.1 %collective-permute-start.27 = (bf16[64,2048]{1,0:T(8,128)(2,1)}, bf16[64,2048]{1,0:T(8,128)(2,1)}, u32[]{:S(2)}, u32[]{:S(2)}) collective-permute-start(bf16[64,2048]{1,0:T(8,128)(2,1)} %get-tuple-element.269), channel_id=1, source_target_pairs={{0,24},{2,26},{4,28},{6,30},{8,0},{10,2},{12,4},{14,6},{16,8},{18,... | collective-permute-start | bytes 786440 | tf_op jit(solution)/shard_map/ppermute | solution.py:366
  283.3 48.2 %collective-permute-start.26 = (bf16[64,2048]{1,0:T(8,128)(2,1)}, bf16[64,2048]{1,0:T(8,128)(2,1)}, u32[]{:S(2)}, u32[]{:S(2)}) collective-permute-start(bf16[64,2048]{1,0:T(8,128)(2,1)} %get-tuple-element.270), channel_id=1, source_target_pairs={{0,16},{2,18},{4,20},{6,22},{8,24},{10,26},{12,28},{14,30},{16,0},... | collective-permute-start | bytes 786440 | tf_op jit(solution)/shard_map/ppermute | solution.py:366
  284.1 49.1 %collective-permute-start.25 = (bf16[64,2048]{1,0:T(8,128)(2,1)}, bf16[64,2048]{1,0:T(8,128)(2,1)}, u32[]{:S(2)}, u32[]{:S(2)}) collective-permute-start(bf16[64,2048]{1,0:T(8,128)(2,1)} %get-tuple-element.271), channel_id=1, source_target_pairs={{0,8},{2,10},{4,12},{6,14},{8,16},{10,18},{12,20},{14,22},{16,24},... | collective-permute-start | bytes 786440 | tf_op jit(solution)/shard_map/ppermute | solution.py:366
  299.8 17.3 %all-to-all-start.2 = ((bf16[16,2,192]{2,1,0:T(2,128)(2,1)}), bf16[16,2,192]{2,1,0:T(2,128)(2,1)S(1)}, u32[]{:S(2)}, u32[]{:S(2)}) async-start(bf16[16,2,192]{2,1,0:T(2,128)(2,1)} %reshape.134), calls=%async_computation.2 | async-start | bytes 32768 | tf_op jit(solution)/shard_map/all_to_all | solution.py:590
  306.3 29.6 %collective-permute-start.23 = (bf16[64,768]{1,0:T(8,128)(2,1)}, bf16[64,768]{1,0:T(8,128)(2,1)}, u32[]{:S(2)}, u32[]{:S(2)}) collective-permute-start(bf16[64,768]{1,0:T(8,128)(2,1)} %get-tuple-element.285), channel_id=1, source_target_pairs={{0,24},{2,26},{4,28},{6,30},{8,0},{10,2},{12,4},{14,6},{16,8},{18,... | collective-permute-start | bytes 294920 | tf_op jit(solution)/shard_map/ppermute | solution.py:366
  311.6 31.4 %collective-permute-start.24 = (bf16[512,1024]{1,0:T(8,128)(2,1)}, bf16[512,1024]{1,0:T(8,128)(2,1)}, u32[]{:S(2)}, u32[]{:S(2)}) collective-permute-start(bf16[512,1024]{1,0:T(8,128)(2,1)} %copy-done.45), channel_id=1, source_target_pairs={{0,1},{1,0},{2,3},{3,2},{4,5},{5,4},{6,7},{7,6},{8,9},{9,8},{10,11... | collective-permute-start | bytes 3145736 | tf_op jit(solution)/shard_map/ppermute | solution.py:329
  323.8 18.9 %collective-permute-start.22 = (bf16[64,768]{1,0:T(8,128)(2,1)S(1)}, bf16[64,768]{1,0:T(8,128)(2,1)}, u32[]{:S(2)}, u32[]{:S(2)}) collective-permute-start(bf16[64,768]{1,0:T(8,128)(2,1)S(1)} %copy-done.71), channel_id=1, source_target_pairs={{0,16},{2,18},{4,20},{6,22},{8,24},{10,26},{12,28},{14,30},{16,0},... | collective-permute-start | bytes 294920 | tf_op jit(solution)/shard_map/ppermute | solution.py:366
  333.2 46.5 %collective-permute-start.30 = (bf16[64,1792]{1,0:T(8,128)(2,1)}, bf16[64,1792]{1,0:T(8,128)(2,1)}, u32[]{:S(2)}, u32[]{:S(2)}) collective-permute-start(bf16[64,1792]{1,0:T(8,128)(2,1)} %get-tuple-element.280), channel_id=1, source_target_pairs={{0,24},{2,26},{4,28},{6,30},{8,0},{10,2},{12,4},{14,6},{16,8},{18,... | collective-permute-start | bytes 688136 | tf_op jit(solution)/shard_map/ppermute | solution.py:366
  335.9 43.8 %collective-permute-start.29 = (bf16[64,1792]{1,0:T(8,128)(2,1)}, bf16[64,1792]{1,0:T(8,128)(2,1)}, u32[]{:S(2)}, u32[]{:S(2)}) collective-permute-start(bf16[64,1792]{1,0:T(8,128)(2,1)} %get-tuple-element.281), channel_id=1, source_target_pairs={{0,16},{2,18},{4,20},{6,22},{8,24},{10,26},{12,28},{14,30},{16,0},... | collective-permute-start | bytes 688136 | tf_op jit(solution)/shard_map/ppermute | solution.py:366
  342.7 36.9 %collective-permute-start.28 = (bf16[64,1792]{1,0:T(8,128)(2,1)}, bf16[64,1792]{1,0:T(8,128)(2,1)}, u32[]{:S(2)}, u32[]{:S(2)}) collective-permute-start(bf16[64,1792]{1,0:T(8,128)(2,1)} %get-tuple-element.282), channel_id=1, source_target_pairs={{0,8},{2,10},{4,12},{6,14},{8,16},{10,18},{12,20},{14,22},{16,24},... | collective-permute-start | bytes 688136 | tf_op jit(solution)/shard_map/ppermute | solution.py:366
  361.6 15.6 %all-to-all-start.3 = ((bf16[16,2,512]{2,1,0:T(2,128)(2,1)}), bf16[16,2,512]{2,1,0:T(2,128)(2,1)}, u32[]{:S(2)}, u32[]{:S(2)}) async-start(bf16[16,2,512]{2,1,0:T(2,128)(2,1)} %reshape.136), calls=%async_computation.4 | async-start | bytes 65536 | tf_op jit(solution)/shard_map/all_to_all | solution.py:602
  (91 other events, 851.8 us)
Sparse Core Ops, SparseCore 0:
  10.9 48.7 all-gather.2
  62.5 82.7 all-gather.4
  274.8 82.3 reduce-scatter.1

commit v3 on v2

--- a/solution.py
+++ b/solution.py
@@ -575,7 +575,9 @@
     pair, part, values = after((pair, part, values))
     last_terms = scatter_x(pair, part)
     own_grad, peers_grad, sums = hidden_back(values, qkv_half, normed_all, tokens)
-    own_grad, peers_grad, sums, last_terms = after((own_grad, peers_grad, sums, last_terms))
+    own_grad, peers_grad, sums, grad_w_down, up_pieces = after(
+        (own_grad, peers_grad, sums, grad_w_down, up_pieces)
+    )
     branch_two = add_parts(branch_parts[0], branch_sent)
     grad_gate_two = jnp.sum(grad_mixed * branch_two, 0)
 
@@ -586,21 +588,22 @@
     hidden_parts = [own_grad] + [
         peers_grad[r * tokens : (r + 1) * tokens] for r in range(splits - 1)
     ]
-    grad_mod, hidden_parts = after((grad_mod, hidden_parts))
+    grad_mod, hidden_parts, first_terms, out_terms, up_pieces, grad_w_down = after(
+        (grad_mod, hidden_parts, first_terms, out_terms, up_pieces, grad_w_down)
+    )
     grad_mod_cols = lax.all_to_all(grad_mod, "fsdp", split_axis=1, concat_axis=0, tiled=True)
     hidden_sent = send_parts(hidden_parts)
+    grad_mod_cols, last_terms = after((grad_mod_cols, last_terms))
     last_pieces = scatter_z(last_terms)
-    grad_mod_cols, first_terms, out_terms = after((grad_mod_cols, first_terms, out_terms))
     joint_pieces = scatter_z(*([out_terms, first_terms] if groups > 1 else [out_terms]))
     grad_w_ada = mm(cond_all, grad_mod_cols, TN)
     grad_b_ada = jnp.sum(grad_mod_cols.astype(wide), 0)
     cond_term = mm(grad_mod_cols, w_ada, NT).astype(low)
-    cond_term, middle, grad_w_down, last_pieces, hidden_sent, up_pieces = after(
-        (cond_term, middle, grad_w_down, last_pieces, hidden_sent, up_pieces)
+    cond_term, middle, grad_w_down, up_pieces, last_pieces, joint_pieces, hidden_sent = after(
+        (cond_term, middle, grad_w_down, up_pieces, last_pieces, joint_pieces, hidden_sent)
     )
     mixed = (middle + gate_two * branch_two).astype(low)
     cond_terms = lax.all_to_all(cond_term, "fsdp", split_axis=0, concat_axis=0, tiled=True)
-    cond_terms, joint_pieces = after((cond_terms, joint_pieces))
     grad_w_up = scatter_end(up_pieces)
     grad_joint = scatter_end(joint_pieces).astype(low)
     grad_w_out = seq_sum(grad_joint[:, :width])

time: 408 us -> 409 us (level)
  waiting for transfers between devices: 90.7 us -> 97 us
  local copies, waits for them, and re-layouts: 44.1 us -> 39.2 us
    ppermute x12, waiting for transfers between devices: 8.98 us -> 27.7 us  [z_send(): lax.ppermute(value, 'fsdp', [(i, (i + 4 * step) % shards) for i in range(...]
    reduce_scatter x1, waiting for transfers between devices: 14.1 us -> 0.01 us  [per_device(): lax.psum_scatter(term_down, 'fsdp', scatter_dimension=0, tiled=True)]
    ppermute x5, waiting for transfers between devices: 10.6 us -> 19.5 us  [x_swap(): return lax.ppermute(value, 'fsdp', [(i, i ^ 2) for i in range(shards)])]
    all_to_all x1, waiting for transfers between devices: 4.77 us -> 0.01 us  [per_device(): lax.all_to_all(grad_mod, 'fsdp', split_axis=1, concat_axis=0, tiled=True)]
    unnamed x167 -> x164, local copies, waits for them, and re-layouts: 36.1 us -> 34.7 us
  transfers between devices with their start and end apart: 39 -> 39, of which waited for: 15 -> 16; matrix products, arithmetic and copies ran while one was open for 20% -> 17% of each run, Pallas kernels for 22% -> 23%
where the time goes in v3:
time: 409 us; the launch traced here: 404 us
  Pallas kernels  109 us (27%)
  waiting for transfers between devices  97 us (24%)
  other arithmetic  59.8 us (15%)
  starting transfers between devices  58.1 us (14%)
  local copies, waits for them, and re-layouts  39.2 us (10%)
  between operations  15.5 us (4%)
  matrix products  13.6 us (3%)
  blocking collectives  12.4 us (3%)
    unnamed x164, local copies, waits for them, and re-layouts  34.7 us
    pallas_call x2, Pallas kernels, feed(): pl.pallas_call(partial(feed_kernel, int(aliased)), grid=(count,), in_spec...  28.8 us
    ppermute x12, waiting for transfers between devices, z_send(): lax.ppermute(value, 'fsdp', [(i, (i + 4 * step) % shards) for i in range(...  27.7 us
    pallas_call x2, Pallas kernels, attend_back(): pl.pallas_call(partial(attend_back_kernel, len(grad_pieces)), grid=(pairs...  25.4 us
    ppermute x12, starting transfers between devices, z_send(): lax.ppermute(value, 'fsdp', [(i, (i + 4 * step) % shards) for i in range(...  23.5 us
    pallas_call x9, Pallas kernels, mat(): pl.pallas_call(mat_turned_kernel if turned else mat_kernel, grid=(columns...  23.4 us
    all_gather x1, waiting for transfers between devices, per_device(): lax.all_gather(jnp.concatenate([up_shard, down_shard.T], 1), 'fsdp', axis...  21.3 us
    pallas_call x2, Pallas kernels, attend(): pl.pallas_call(attend_kernel, grid=(pairs, count), in_specs=[pl.BlockSpec...  19.9 us
  transfers between devices with their start and end apart: 39, of which 16 were waited for; matrix products, arithmetic and copies ran while one was open for 17% of the time, Pallas kernels for 23%

profile of v3, /device:TPU:0, one launch (start us, length us, event | category | flops | bytes accessed | tf_op | source)
XLA Modules:
  0.0 404.3 jit_solution(36589002574254887)
XLA Ops:
  14.8 12.4 %all_to_all.47 = bf16[16,2,512]{2,1,0:T(2,128)(2,1)S(1)} all-to-all(bf16[16,2,512]{2,1,0:T(2,128)(2,1)S(1)} %reshape.131), channel_id=1, replica_groups=mesh['fsdp'=16,'seq'=2] {'fsdp'}, dimensions={0} | all-to-all | bytes 65536 | tf_op jit(solution)/shard_map/all_to_all | solution.py:424
  27.3 8.2 %collective-permute-done = bf16[512,1024]{1,0:T(8,128)(2,1)S(1)} collective-permute-done((bf16[512,1024]{1,0:T(8,128)(2,1)}, bf16[512,1024]{1,0:T(8,128)(2,1)S(1)}, u32[]{:S(2)}, u32[]{:S(2)}) %collective-permute-start) | collective-permute-done | bytes 1048608 | tf_op jit(solution)/shard_map/ppermute | solution.py:326
  41.1 5.9 %all-to-all-start.1 = ((bf16[16,2,192]{2,1,0:T(2,128)(2,1)}), bf16[16,2,192]{2,1,0:T(2,128)(2,1)S(1)}, u32[]{:S(2)}, u32[]{:S(2)}) async-start(bf16[16,2,192]{2,1,0:T(2,128)(2,1)} %reshape.133), calls=%async_computation.1 | async-start | bytes 32768 | tf_op jit(solution)/shard_map/all_to_all | solution.py:434
  48.2 5.3 %all-to-all-done.1 = bf16[16,2,192]{2,1,0:T(2,128)(2,1)S(1)} async-done(((bf16[16,2,192]{2,1,0:T(2,128)(2,1)}), bf16[16,2,192]{2,1,0:T(2,128)(2,1)S(1)}, u32[]{:S(2)}, u32[]{:S(2)}) %all-to-all-start.1) | async-done | bytes 12320 | tf_op jit(solution)/shard_map/all_to_all | solution.py:434
  56.2 4.6 %fusion = (f32[1024,1024]{1,0:T(8,128)}, bf16[1024,1024]{1,0:T(8,128)(2,1)S(1)}) fusion(f32[1024]{0:T(1024)S(1)} %add_rsqrt_fusion, f32[1024]{0:T(1024)S(1)} %broadcast_multiply_fusion, bf16[512,1024]{1,0:T(8,128)(2,1)} %copy-done.47, bf16[512,1024]{1,0:T(8,128)(2,1)} %bitcast.72, f32[1024]{0:T(1024)S(1)} %bitcast.105, f32[1024]{0:T(1024)S(1)} %bitcast.93), kind=kLoop, calls=%fused_computation.2 | loop fusion | flops 9437184 | bytes 8404992 | tf_op jit(solution)/shard_map/mul | solution.py:32
  60.8 6.2 %convolution_convert_fusion.query_ref.all_ref = bf16[1024,1536]{1,0:T(8,128)(2,1)S(1)} fusion(bf16[1024,1024]{1,0:T(8,128)(2,1)S(1)} %get-tuple-element.284.value_ref, bf16[1024,1536]{1,0:T(8,128)(2,1)} %all-gather.3.cloned.1.call-done.refs_2_), kind=kOutput, calls=%fused_computation.7 | convolution fusion | flops 3222798336 | bytes 8388608 | tf_op jit(solution)/shard_map/dot_general | solution.py:26
  70.1 9.9 %attend.2 = (bf16[512,512]{1,0:T(8,128)(2,1)S(1)}, f32[4,2,512]{2,1,0:T(2,128)S(1)}) custom-call(bf16[1024,1536]{1,0:T(8,128)(2,1)S(1)} %convolution_convert_fusion.query_ref.all_ref, bf16[1024,1536]{1,0:T(8,128)(2,1)S(1)} %convolution_convert_fusion.query_ref.all_ref), custom_call_target="tpu_custom_call" | custom-call | flops 2097152 | tf_op jit(solution)/shard_map/attend/pallas_call | solution.py:68
  83.6 9.9 %attend.3 = (bf16[512,512]{1,0:T(8,128)(2,1)S(1)}, f32[4,2,512]{2,1,0:T(2,128)S(1)}) custom-call(bf16[1024,1536]{1,0:T(8,128)(2,1)S(1)} %copy-done.2, bf16[1024,1536]{1,0:T(8,128)(2,1)S(1)} %copy-done.2), custom_call_target="tpu_custom_call" | custom-call | flops 2097152 | tf_op jit(solution)/shard_map/attend/pallas_call | solution.py:68
  124.0 21.3 %all-gather.5.cloned.1.call-done.up_ref.down_ref = bf16[1024,4096]{1,0:T(8,128)(2,1)} async-done(((bf16[64,4096]{1,0:T(8,128)(2,1)}), bf16[1024,4096]{1,0:T(8,128)(2,1)}) %all-gather.5.cloned.1.call-update) | async-done | bytes 8388624 | tf_op jit(solution)/shard_map/all_gather | solution.py:446
  148.2 14.6 %feed.2 = (bf16[1024,2048]{1,0:T(8,128)(2,1)S(1)}, bf16[1024,2048]{1,0:T(8,128)(2,1)S(1)}, bf16[512,1024]{1,0:T(8,128)(2,1)S(1)}, bf16[512,1024]{1,0:T(8,128)(2,1)}) custom-call(bf16[512,1024]{1,0:T(8,128)(2,1)S(1)} %copy-done.24, bf16[1024,1024]{1,0:T(8,128)(2,1)S(1)} %copy-done.9, bf16[1024,4096]{1,0:T(8,128)(2,1)} %all-gather.5.cloned.1.call-done.up_ref.down_ref, ...), custom_call_target="tpu_custom_call" | custom-call | flops 1048576 | tf_op jit(solution)/shard_map/feed/pallas_call | solution.py:135
  166.2 14.1 %feed.3 = (bf16[1024,2048]{1,0:T(8,128)(2,1)S(1)}, bf16[1024,2048]{1,0:T(8,128)(2,1)}, f32[512,1024]{1,0:T(8,128)S(1)}, f32[512,1024]{1,0:T(8,128)S(1)}) custom-call(bf16[512,1024]{1,0:T(8,128)(2,1)S(1)} %copy-done.16, bf16[1024,1024]{1,0:T(8,128)(2,1)S(1)} %copy-done.10, ...), custom_call_target="tpu_custom_call", output_to_operand_aliasing={{0}: (4, {}), {1}: (5, {})} | custom-call | flops 1048576 | tf_op jit(solution)/shard_map/feed/pallas_call | solution.py:135
  183.0 6.3 %mat.9 = bf16[1024,2048]{1,0:T(8,128)(2,1)S(1)} custom-call(bf16[1024,1024]{1,0:T(8,128)(2,1)S(1)} %copy-done.10, bf16[1024,2048]{1,0:T(8,128)(2,1)S(1)} %get-tuple-element.171.right_ref), custom_call_target="tpu_custom_call" | custom-call | flops 1048576 | tf_op jit(solution)/shard_map/mat/pallas_call | solution.py:205
  195.2 4.1 %mat.11 = bf16[512,2048]{1,0:T(8,128)(2,1)} custom-call(bf16[1024,1024]{1,0:T(8,128)(2,1)S(1)} %copy-done.12, bf16[1024,2048]{1,0:T(8,128)(2,1)S(1)} %copy-done.5), custom_call_target="tpu_custom_call" | custom-call | flops 524288 | tf_op jit(solution)/shard_map/mat/pallas_call | solution.py:205
  223.3 5.3 %collective-permute-done.12.rest_1_ = bf16[512,512]{1,0:T(8,128)(2,1)S(1)} collective-permute-done((bf16[512,512]{1,0:T(8,128)(2,1)S(1)}, bf16[512,512]{1,0:T(8,128)(2,1)S(1)}, u32[]{:S(2)}, u32[]{:S(2)}) %collective-permute-start.12) | collective-permute-done | bytes 524320 | tf_op jit(solution)/shard_map/ppermute | solution.py:329
  229.3 12.6 %attend_back.2.right_ref.refs_0_ = bf16[1024,768]{1,0:T(8,128)(2,1)S(1)} custom-call(bf16[1024,1536]{1,0:T(8,128)(2,1)S(1)} %copy-done.3, f32[4,2,1024]{2,1,0:T(2,128)S(1)} %constant_dynamic-update-slice_fusion.lse_ref, bf16[512,512]{1,0:T(8,128)(2,1)S(1)} %get-tuple-element.186.rest_0_, bf16[512,512]{1,0:T(8,128)(2,1)S(1)} %collective-permute-done.12.rest_1_), custom_call_target="tpu_custom_call" | custom-call | flops 2097152 | tf_op jit(solution)/shard_map/attend_back/pallas_call | solution.py:293
  247.5 10.7 %collective-permute-done.14 = bf16[256,2048]{1,0:T(8,128)(2,1)S(1)} collective-permute-done((bf16[256,2048]{1,0:T(8,128)(2,1)S(1)}, bf16[256,2048]{1,0:T(8,128)(2,1)S(1)}, u32[]{:S(2)}, u32[]{:S(2)}) %collective-permute-start.14) | collective-permute-done | bytes 1048608 | tf_op jit(solution)/shard_map/ppermute | solution.py:363
  258.5 12.8 %attend_back.3.right_ref.refs_1_ = bf16[1024,768]{1,0:T(8,128)(2,1)S(1)} custom-call(bf16[1024,1536]{1,0:T(8,128)(2,1)S(1)} %copy-done.3, f32[4,2,1024]{2,1,0:T(2,128)S(1)} %constant_dynamic-update-slice_fusion.lse_ref, bf16[512,512]{1,0:T(8,128)(2,1)S(1)} %get-tuple-element.186.rest_0_, bf16[512,512]{1,0:T(8,128)(2,1)S(1)} %collective-permute-done.12.rest_1_), custom_call_target="tpu_custom_call" | custom-call | flops 2097152 | tf_op jit(solution)/shard_map/attend_back/pallas_call | solution.py:293
  272.3 7.9 %collective-permute-done.15 = bf16[256,768]{1,0:T(8,128)(2,1)S(1)} collective-permute-done((bf16[256,768]{1,0:T(8,128)(2,1)S(1)}, bf16[256,768]{1,0:T(8,128)(2,1)S(1)}, u32[]{:S(2)}, u32[]{:S(2)}) %collective-permute-start.15) | collective-permute-done | bytes 393248 | tf_op jit(solution)/shard_map/ppermute | solution.py:363
  293.7 5.3 %hidden_back.1 = (f32[512,1024]{1,0:T(8,128)S(1)}, bf16[512,1024]{1,0:T(8,128)(2,1)}, f32[2,1024]{1,0:T(2,128)S(1)}) custom-call(bf16[1024,768]{1,0:T(8,128)(2,1)S(1)} %attend_back.2.right_ref.refs_0_, bf16[1024,768]{1,0:T(8,128)(2,1)S(1)} %attend_back.3.right_ref.refs_1_, bf16[1024,1536]{1,0:T(8,128)(2,1)S(1)} %copy-done.34, f32[1024,1024]{1,0:T(8,128)S(1)} %copy-done.7), custom_call_target="tpu_custom_call" | custom-call | flops 1048576 | tf_op jit(solution)/shard_map/hidden_back/pallas_call | solution.py:238
  299.8 11.4 %collective-permute-done.20 = bf16[64,2048]{1,0:T(8,128)(2,1)S(1)} collective-permute-done((bf16[64,2048]{1,0:T(8,128)(2,1)S(1)}, bf16[64,2048]{1,0:T(8,128)(2,1)S(1)}, u32[]{:S(2)}, u32[]{:S(2)}) %collective-permute-start.20) | collective-permute-done | bytes 262176 | tf_op jit(solution)/shard_map/ppermute | solution.py:366
  337.9 8.9 %collective-permute-done.26 = bf16[64,768]{1,0:T(8,128)(2,1)S(1)} collective-permute-done((bf16[64,768]{1,0:T(8,128)(2,1)S(1)}, bf16[64,768]{1,0:T(8,128)(2,1)S(1)}, u32[]{:S(2)}, u32[]{:S(2)}) %collective-permute-start.26) | collective-permute-done | bytes 98336 | tf_op jit(solution)/shard_map/ppermute | solution.py:366
  346.7 4.7 %collective-permute-start.25 = (bf16[64,768]{1,0:T(8,128)(2,1)S(1)}, bf16[64,768]{1,0:T(8,128)(2,1)S(1)}, u32[]{:S(2)}, u32[]{:S(2)}) collective-permute-start(bf16[64,768]{1,0:T(8,128)(2,1)S(1)} %get-tuple-element.304), channel_id=1, source_target_pairs={{0,16},{2,18},{4,20},{6,22},{8,24},{10,26},{12,28},{14,30},{16,0},... | collective-permute-start | bytes 294920 | tf_op jit(solution)/shard_map/ppermute | solution.py:366
  354.0 4.2 %collective-permute-start.24 = (bf16[64,768]{1,0:T(8,128)(2,1)S(1)}, bf16[64,768]{1,0:T(8,128)(2,1)S(1)}, u32[]{:S(2)}, u32[]{:S(2)}) collective-permute-start(bf16[64,768]{1,0:T(8,128)(2,1)S(1)} %get-tuple-element.305), channel_id=1, source_target_pairs={{0,8},{2,10},{4,12},{6,14},{8,16},{10,18},{12,20},{14,22},{16,24},... | collective-permute-start | bytes 294920 | tf_op jit(solution)/shard_map/ppermute | solution.py:366
  367.4 4.1 %all-to-all-start.3 = ((bf16[16,2,512]{2,1,0:T(2,128)(2,1)}), bf16[16,2,512]{2,1,0:T(2,128)(2,1)S(1)}, u32[]{:S(2)}, u32[]{:S(2)}) async-start(bf16[16,2,512]{2,1,0:T(2,128)(2,1)} %reshape.137), calls=%async_computation.4 | async-start | bytes 65536 | tf_op jit(solution)/shard_map/all_to_all | solution.py:606
  (334 shorter events, 178.0 us)
Async XLA Ops:
  7.2 53.6 %all-gather.3.cloned.1.call-start = ((), (), s32[]{:S(2)}) async-start(), calls=%async_computation.5 | async-start | bytes 3342336 | tf_op jit(solution)/shard_map/all_gather | solution.py:444
  9.0 136.3 %all-gather.5.cloned.1.call-start = ((), (), s32[]{:S(2)}) async-start(), calls=%async_computation.6 | async-start | bytes 8912896 | tf_op jit(solution)/shard_map/all_gather | solution.py:446
  9.1 26.4 %collective-permute-start = (bf16[512,1024]{1,0:T(8,128)(2,1)}, bf16[512,1024]{1,0:T(8,128)(2,1)S(1)}, u32[]{:S(2)}, u32[]{:S(2)}) collective-permute-start(bf16[512,1024]{1,0:T(8,128)(2,1)} %bitcast.71), channel_id=1, source_target_pairs={{1,0},{0,1},{3,2},{2,3},{5,4},{4,5},{7,6},{6,7},{9,8},{8,9},{11,10... | collective-permute-start | bytes 3145736 | tf_op jit(solution)/shard_map/ppermute | solution.py:326
  37.7 42.3 %collective-permute-start.4 = (bf16[512,1024]{1,0:T(8,128)(2,1)}, bf16[512,1024]{1,0:T(8,128)(2,1)}, u32[]{:S(2)}, u32[]{:S(2)}) collective-permute-start(bf16[512,1024]{1,0:T(8,128)(2,1)} %bitcast.6), channel_id=1, source_target_pairs={{1,0},{0,1},{3,2},{2,3},{5,4},{4,5},{7,6},{6,7},{9,8},{8,9},{11,10... | collective-permute-start | bytes 3145736 | tf_op jit(solution)/shard_map/ppermute | solution.py:326
  47.0 264.8 %reduce-scatter.2.cloned.1.call-start = ((), (), s32[]{:S(2)}) async-start(), calls=%async_computation.7 | async-start | bytes 4456448 | tf_op jit(solution)/shard_map/reduce_scatter | solution.py:525
  54.2 15.1 %collective-permute-start.2 = (bf16[64,1024]{1,0:T(8,128)(2,1)S(1)}, bf16[64,1024]{1,0:T(8,128)(2,1)S(1)}, u32[]{:S(2)}, u32[]{:S(2)}) collective-permute-start(bf16[64,1024]{1,0:T(8,128)(2,1)S(1)} %copy-done.64), channel_id=1, source_target_pairs={{0,16},{2,18},{4,20},{6,22},{8,24},{10,26},{12,28},{14,30},{16,0},... | collective-permute-start | bytes 393224 | tf_op jit(solution)/shard_map/ppermute | solution.py:366
  69.5 24.1 %collective-permute-start.5 = (bf16[4,64,1024]{2,1,0:T(8,128)(2,1)S(1)}, bf16[4,64,1024]{2,1,0:T(8,128)(2,1)S(1)}, u32[]{:S(2)}, u32[]{:S(2)}) collective-permute-start(bf16[4,64,1024]{2,1,0:T(8,128)(2,1)S(1)} %bitcast_dynamic-update-slice_fusion), channel_id=1, source_target_pairs={{0,4},{2,6},{4,0},{6,2},{8,12},{10,14},{12,8},{14,10},{16,20},{18,... | collective-permute-start | bytes 1572872 | tf_op jit(solution)/shard_map/ppermute | solution.py:363
  102.9 14.3 %collective-permute-start.8 = (bf16[512,512]{1,0:T(8,128)(2,1)S(1)}, bf16[512,512]{1,0:T(8,128)(2,1)S(1)}, u32[]{:S(2)}, u32[]{:S(2)}) collective-permute-start(bf16[512,512]{1,0:T(8,128)(2,1)S(1)} %copy-done.38), channel_id=1, source_target_pairs={{1,0},{0,1},{3,2},{2,3},{5,4},{4,5},{7,6},{6,7},{9,8},{8,9},{11,10... | collective-permute-start | bytes 1572872 | tf_op jit(solution)/shard_map/ppermute | solution.py:326
  164.7 26.6 %collective-permute-start.9 = (bf16[512,1024]{1,0:T(8,128)(2,1)}, bf16[512,1024]{1,0:T(8,128)(2,1)}, u32[]{:S(2)}, u32[]{:S(2)}) collective-permute-start(bf16[512,1024]{1,0:T(8,128)(2,1)} %get-tuple-element.170), channel_id=1, source_target_pairs={{0,1},{1,0},{2,3},{3,2},{4,5},{5,4},{6,7},{7,6},{8,9},{9,8},{10,11... | collective-permute-start | bytes 3145736 | tf_op jit(solution)/shard_map/ppermute | solution.py:329
  199.3 22.2 %collective-permute-start.10 = (bf16[512,2048]{1,0:T(8,128)(2,1)}, bf16[512,2048]{1,0:T(8,128)(2,1)}, u32[]{:S(2)}, u32[]{:S(2)}) collective-permute-start(bf16[512,2048]{1,0:T(8,128)(2,1)} %mat.11), channel_id=1, source_target_pairs={{0,2},{2,0},{4,6},{6,4},{8,10},{10,8},{12,14},{14,12},{16,18},{18,... | collective-permute-start | bytes 6291464 | tf_op jit(solution)/shard_map/ppermute | solution.py:360
  228.7 29.5 %collective-permute-start.14 = (bf16[256,2048]{1,0:T(8,128)(2,1)S(1)}, bf16[256,2048]{1,0:T(8,128)(2,1)S(1)}, u32[]{:S(2)}, u32[]{:S(2)}) collective-permute-start(bf16[256,2048]{1,0:T(8,128)(2,1)S(1)} %add_convert_fusion.2), channel_id=1, source_target_pairs={{0,4},{2,6},{4,0},{6,2},{8,12},{10,14},{12,8},{14,10},{16,20},{18,... | collective-permute-start | bytes 3145736 | tf_op jit(solution)/shard_map/ppermute | solution.py:363
  243.6 28.6 %collective-permute-start.17 = (bf16[512,1024]{1,0:T(8,128)(2,1)S(1)}, bf16[512,1024]{1,0:T(8,128)(2,1)S(1)}, u32[]{:S(2)}, u32[]{:S(2)}) collective-permute-start(bf16[512,1024]{1,0:T(8,128)(2,1)S(1)} %copy-done.40), channel_id=1, source_target_pairs={{0,1},{1,0},{2,3},{3,2},{4,5},{5,4},{6,7},{7,6},{8,9},{9,8},{10,11... | collective-permute-start | bytes 3145736 | tf_op jit(solution)/shard_map/ppermute | solution.py:329
  244.3 28.0 %collective-permute-start.16 = (bf16[256,1024]{1,0:T(8,128)(2,1)S(1)}, bf16[256,1024]{1,0:T(8,128)(2,1)S(1)}, u32[]{:S(2)}, u32[]{:S(2)}) collective-permute-start(bf16[256,1024]{1,0:T(8,128)(2,1)S(1)} %add_convert_fusion.5), channel_id=1, source_target_pairs={{0,4},{2,6},{4,0},{6,2},{8,12},{10,14},{12,8},{14,10},{16,20},{18,... | collective-permute-start | bytes 1572872 | tf_op jit(solution)/shard_map/ppermute | solution.py:363
  258.2 21.9 %collective-permute-start.15 = (bf16[256,768]{1,0:T(8,128)(2,1)S(1)}, bf16[256,768]{1,0:T(8,128)(2,1)S(1)}, u32[]{:S(2)}, u32[]{:S(2)}) collective-permute-start(bf16[256,768]{1,0:T(8,128)(2,1)S(1)} %add_convert_fusion.7), channel_id=1, source_target_pairs={{0,4},{2,6},{4,0},{6,2},{8,12},{10,14},{12,8},{14,10},{16,20},{18,... | collective-permute-start | bytes 1179656 | tf_op jit(solution)/shard_map/ppermute | solution.py:363
  284.6 14.4 %collective-permute-start.21 = (bf16[64,2048]{1,0:T(8,128)(2,1)S(1)}, bf16[64,2048]{1,0:T(8,128)(2,1)S(1)}, u32[]{:S(2)}, u32[]{:S(2)}) collective-permute-start(bf16[64,2048]{1,0:T(8,128)(2,1)S(1)} %get-tuple-element.287), channel_id=1, source_target_pairs={{0,24},{2,26},{4,28},{6,30},{8,0},{10,2},{12,4},{14,6},{16,8},{18,... | collective-permute-start | bytes 786440 | tf_op jit(solution)/shard_map/ppermute | solution.py:366
  288.0 23.1 %collective-permute-start.20 = (bf16[64,2048]{1,0:T(8,128)(2,1)S(1)}, bf16[64,2048]{1,0:T(8,128)(2,1)S(1)}, u32[]{:S(2)}, u32[]{:S(2)}) collective-permute-start(bf16[64,2048]{1,0:T(8,128)(2,1)S(1)} %get-tuple-element.288), channel_id=1, source_target_pairs={{0,16},{2,18},{4,20},{6,22},{8,24},{10,26},{12,28},{14,30},{16,0},... | collective-permute-start | bytes 786440 | tf_op jit(solution)/shard_map/ppermute | solution.py:366
  288.0 23.9 %collective-permute-start.19 = (bf16[64,2048]{1,0:T(8,128)(2,1)S(1)}, bf16[64,2048]{1,0:T(8,128)(2,1)}, u32[]{:S(2)}, u32[]{:S(2)}) collective-permute-start(bf16[64,2048]{1,0:T(8,128)(2,1)S(1)} %get-tuple-element.289), channel_id=1, source_target_pairs={{0,8},{2,10},{4,12},{6,14},{8,16},{10,18},{12,20},{14,22},{16,24},... | collective-permute-start | bytes 786440 | tf_op jit(solution)/shard_map/ppermute | solution.py:366
  313.5 18.5 %collective-permute-start.23 = (bf16[256,768]{1,0:T(8,128)(2,1)}, bf16[256,768]{1,0:T(8,128)(2,1)}, u32[]{:S(2)}, u32[]{:S(2)}) collective-permute-start(bf16[256,768]{1,0:T(8,128)(2,1)} %add_convert_fusion.6), channel_id=1, source_target_pairs={{0,4},{2,6},{4,0},{6,2},{8,12},{10,14},{12,8},{14,10},{16,20},{18,... | collective-permute-start | bytes 1179656 | tf_op jit(solution)/shard_map/ppermute | solution.py:363
  317.2 14.6 %all-to-all-start.2 = ((bf16[16,2,192]{2,1,0:T(2,128)(2,1)}), bf16[16,2,192]{2,1,0:T(2,128)(2,1)S(1)}, u32[]{:S(2)}, u32[]{:S(2)}) async-start(bf16[16,2,192]{2,1,0:T(2,128)(2,1)} %reshape.135), calls=%async_computation.3 | async-start | bytes 32768 | tf_op jit(solution)/shard_map/all_to_all | solution.py:594
  325.5 36.9 %collective-permute-start.29 = (bf16[64,1792]{1,0:T(8,128)(2,1)}, bf16[64,1792]{1,0:T(8,128)(2,1)}, u32[]{:S(2)}, u32[]{:S(2)}) collective-permute-start(bf16[64,1792]{1,0:T(8,128)(2,1)} %get-tuple-element.298), channel_id=1, source_target_pairs={{0,24},{2,26},{4,28},{6,30},{8,0},{10,2},{12,4},{14,6},{16,8},{18,... | collective-permute-start | bytes 688136 | tf_op jit(solution)/shard_map/ppermute | solution.py:366
  329.3 33.8 %collective-permute-start.28 = (bf16[64,1792]{1,0:T(8,128)(2,1)}, bf16[64,1792]{1,0:T(8,128)(2,1)}, u32[]{:S(2)}, u32[]{:S(2)}) collective-permute-start(bf16[64,1792]{1,0:T(8,128)(2,1)} %get-tuple-element.299), channel_id=1, source_target_pairs={{0,16},{2,18},{4,20},{6,22},{8,24},{10,26},{12,28},{14,30},{16,0},... | collective-permute-start | bytes 688136 | tf_op jit(solution)/shard_map/ppermute | solution.py:366
  329.3 33.8 %collective-permute-start.27 = (bf16[64,1792]{1,0:T(8,128)(2,1)}, bf16[64,1792]{1,0:T(8,128)(2,1)}, u32[]{:S(2)}, u32[]{:S(2)}) collective-permute-start(bf16[64,1792]{1,0:T(8,128)(2,1)} %get-tuple-element.300), channel_id=1, source_target_pairs={{0,8},{2,10},{4,12},{6,14},{8,16},{10,18},{12,20},{14,22},{16,24},... | collective-permute-start | bytes 688136 | tf_op jit(solution)/shard_map/ppermute | solution.py:366
  330.4 32.7 %collective-permute-start.30 = (bf16[512,1024]{1,0:T(8,128)(2,1)}, bf16[512,1024]{1,0:T(8,128)(2,1)}, u32[]{:S(2)}, u32[]{:S(2)}) collective-permute-start(bf16[512,1024]{1,0:T(8,128)(2,1)} %get-tuple-element.241), channel_id=1, source_target_pairs={{0,1},{1,0},{2,3},{3,2},{4,5},{5,4},{6,7},{7,6},{8,9},{9,8},{10,11... | collective-permute-start | bytes 3145736 | tf_op jit(solution)/shard_map/ppermute | solution.py:329
  367.4 15.1 %all-to-all-start.3 = ((bf16[16,2,512]{2,1,0:T(2,128)(2,1)}), bf16[16,2,512]{2,1,0:T(2,128)(2,1)S(1)}, u32[]{:S(2)}, u32[]{:S(2)}) async-start(bf16[16,2,512]{2,1,0:T(2,128)(2,1)} %reshape.137), calls=%async_computation.4 | async-start | bytes 65536 | tf_op jit(solution)/shard_map/all_to_all | solution.py:606
  (90 other events, 910.6 us)
Sparse Core Ops, SparseCore 0:
  10.9 48.9 all-gather.2
  62.6 82.6 all-gather.4
  191.5 82.7 reduce-scatter.1
